TPU v7x, 32 devices: a whole 2x2x4 slice. The times are simulated.
32 devices in a mesh: dom: 8 (over z, y), scen: 4 (over x, core).
Axes of the slice: x: 2, y: 2, z: 4, core: 2. Of those that a mesh axis runs over, the one named last changes fastest.
Arguments:
- embedding: bfloat16 [81920, 256], P(('dom', 'scen')), may hold values from -6 to 6
- scenario_feats: bfloat16 [16, 81920], P(None, ('dom', 'scen')), may hold values from -6 to 6
- adjacency: bfloat16 [640, 2, 128, 128], P(('dom', 'scen')), may hold values from -0.3125 to 0.3125
- driver_weight: bfloat16 [81920, 128], P(('dom', 'scen')), may hold values from -0.3125 to 0.3125
- local_slot: int32 [640], P(('dom', 'scen')), may hold values from 0 to 79, as said below
- halo_slot: int32 [640], P(('dom', 'scen')), may hold values from 0 to 15, as said below
- send_rows: int32 [256, 256], P(('dom', 'scen')), may hold values from 0 to 2559
- send_count: int32 [256], P(('dom', 'scen')), may hold values from 1 to 256, as said below
- hot_ids: int32 [128], replicated, may hold values from 0 to 81919, as said below
- first_weight: bfloat16 [512, 256], P('scen'), may hold values from -0.25 to 0.25
- feature_weight: bfloat16 [16, 256], replicated, may hold values from -1.5 to 1.5
- first_bias: float32 [256], replicated, may hold values from -3 to 3
- second_weight: bfloat16 [256, 256], P('scen'), may hold values from -0.375 to 0.375
- second_bias: float32 [256], replicated, may hold values from -3 to 3
Outputs:
- updated: bfloat16 [81920, 256], P(('dom', 'scen'))
Inputs may be any that keep to these rules, and one draw needn't show every extreme that they name: `local_slot`: the 20 entries of one device are distinct and name exactly 5 tiles of each device of its partition; values s * 20 to s * 20 + 19 are tiles of scen index s. `halo_slot`: the entries of one device name every halo tile at least once. `send_count`: every device has a partition to which it sends 256 pins. `hot_ids`: no device holds more than 4 of them, and some device holds exactly that many.
All inputs are finite; a program needn't handle non-finite values.
Results may differ from a plain program's by a relative error of at most 0.0038.
Values may be sent and summed in bfloat16 or wider, within the bound.
A program may use at most 64 MiB of HBM per device.

v0:
```python
import jax
import jax.numpy as jnp
from jax import lax
from jax.sharding import PartitionSpec as P


def per_device(
    embedding,
    scenario_feats,
    adjacency,
    driver_weight,
    local_slot,
    halo_slot,
    send_rows,
    send_count,
    hot_ids,
    first_weight,
    feature_weight,
    first_bias,
    second_weight,
    second_bias,
):
    rows, width = embedding.shape
    tile = adjacency.shape[-1]
    tiles = rows // tile
    groups = lax.axis_size("scen")
    partition = lax.all_gather(embedding, "scen", axis=0, tiled=True)
    local_tiles = partition.reshape(groups * tiles, tile, width)[local_slot]
    slots_per_peer = send_rows.shape[1]
    live = jnp.arange(slots_per_peer, dtype=jnp.int32)[None, :] < send_count[:, None]
    outgoing_rows = jnp.where(
        live[:, :, None], embedding[send_rows], jnp.zeros((), embedding.dtype)
    )
    incoming = lax.all_to_all(outgoing_rows, "dom", split_axis=0, concat_axis=0, tiled=True)
    halo_tiles = incoming.reshape(-1, tile, width)[halo_slot]
    myself = lax.axis_index(("dom", "scen"))
    owner = hot_ids // rows
    within = hot_ids - owner * rows
    mine = jnp.where(
        (owner == myself)[:, None], embedding[within].astype(jnp.float32), jnp.float32(0.0)
    )
    drivers = lax.psum(mine, ("dom", "scen")).astype(jnp.bfloat16)
    summed = jnp.einsum(
        "tij,tjc->tic", adjacency[:, 0], local_tiles, preferred_element_type=jnp.float32
    )
    summed = summed + jnp.einsum(
        "tij,tjc->tic", adjacency[:, 1], halo_tiles, preferred_element_type=jnp.float32
    )
    summed = summed.reshape(rows, width) + jnp.dot(
        driver_weight, drivers, preferred_element_type=jnp.float32
    )
    aggregate = summed.astype(jnp.bfloat16)
    joined = jnp.concatenate([embedding, aggregate], axis=1)
    starting = (
        jnp.dot(scenario_feats.T, feature_weight, preferred_element_type=jnp.float32) + first_bias
    )
    columns = joined
    inner = starting + jnp.dot(
        columns,
        lax.all_gather(first_weight, "scen", axis=0, tiled=True),
        preferred_element_type=jnp.float32,
    )
    activated = jax.nn.gelu(inner, approximate=False).astype(jnp.bfloat16)
    residual = embedding.astype(jnp.float32) + second_bias
    columns = activated
    result = residual + jnp.dot(
        columns,
        lax.all_gather(second_weight, "scen", axis=0, tiled=True),
        preferred_element_type=jnp.float32,
    )
    return result.astype(jnp.bfloat16)


def solution(mesh):
    return jax.shard_map(
        per_device,
        mesh=mesh,
        in_specs=(
            P(("dom", "scen"), None),
            P(None, ("dom", "scen")),
            P(("dom", "scen"), None, None, None),
            P(("dom", "scen"), None),
            P(("dom", "scen")),
            P(("dom", "scen")),
            P(("dom", "scen"), None),
            P(("dom", "scen")),
            P(),
            P("scen", None),
            P(),
            P(),
            P("scen", None),
            P(),
        ),
        out_specs=P(("dom", "scen"), None),
        check_vma=False,
    )
```

profile of v0, /device:TPU:0, one launch (start us, length us, event | category | flops | bytes accessed | tf_op | source)
XLA Modules:
  0.0 112.2 jit_solution(8932517894245466452)
XLA Ops:
  6.5 0.7 all-gather.2.cloned.1.call-update
  7.3 0.7 fusion.57
  8.0 7.5 %gather_fusion.1 = bf16[2048,256]{1,0:T(8,128)(2,1)S(1)} fusion(bf16[2560,256]{1,0:T(8,128)(2,1)S(1)} %copy-done.1, s32[2048]{0:T(1024)S(1)} %broadcast_clamp_fusion), kind=kCustom, calls=%fused_computation.1 | custom fusion | bytes 2105344 | tf_op jit(solution)/shard_map/gather | solution.py:32
  15.5 0.1 iota_compare_fusion
  15.6 1.2 %broadcast_select_fusion = bf16[8,256,256]{2,1,0:T(8,128)(2,1)} fusion(bf16[8,256,256]{2,1,0:T(8,128)(2,1)S(1)} %bitcast.35, pred[8,256]{1,0:T(8,128)(4,1)S(1)} %iota_compare_fusion), kind=kLoop, calls=%fused_computation.64 | loop fusion | flops 524288 | bytes 2099200 | tf_op jit(solution)/shard_map/jit(_where)/select_n | solution.py:31
  16.8 7.3 %all-to-all-start = ((bf16[8,256,256]{2,1,0:T(8,128)(2,1)}), bf16[8,256,256]{2,1,0:T(8,128)(2,1)S(1)}, u32[]{:S(2)}, u32[]{:S(2)}) async-start(bf16[8,256,256]{2,1,0:T(8,128)(2,1)} %broadcast_select_fusion), calls=%async_computation | async-start | bytes 2097152 | tf_op jit(solution)/shard_map/all_to_all | solution.py:34
  24.2 0.8 gather_fusion.3
  25.0 0.1 convert_select_fusion
  25.1 45.3 %all-reduce.1 = bf16[128,256]{1,0:T(8,128)(2,1)S(1)} all-reduce(f32[128,256]{1,0:T(8,128)S(1)} %convert_select_fusion), channel_id=1, replica_groups=mesh['dom'=8,'scen'=4] {'dom','scen'}, use_global_device_ids=true, to_apply=%region_0.1 | all-reduce | flops 32768 | bytes 196608 | tf_op jit(solution)/shard_map/psum | solution.py:42
  70.4 6.0 %all_gather.11 = bf16[256,256]{1,0:T(8,128)(2,1)S(1)} all-gather(bf16[64,256]{1,0:T(8,128)(2,1)} %param.26), channel_id=1, replica_groups=mesh['dom'=8,'scen'=4] {'scen'}, dimensions={0}, use_global_device_ids=true | all-gather | bytes 163840 | tf_op jit(solution)/shard_map/all_gather | solution.py:68
  76.4 6.6 %all_gather.10 = bf16[512,256]{1,0:T(8,128)(2,1)} all-gather(bf16[128,256]{1,0:T(8,128)(2,1)S(1)} %copy-done.5), channel_id=1, replica_groups=mesh['dom'=8,'scen'=4] {'scen'}, dimensions={0}, use_global_device_ids=true | all-gather | bytes 327680 | tf_op jit(solution)/shard_map/all_gather | solution.py:60
  83.0 0.7 compare_select_fusion.2
  83.6 0.7 compare_select_fusion.3
  84.3 0.6 pad_clamp_fusion.2
  84.9 2.7 %convolution_add_fusion.2 = f32[2560,256]{1,0:T(8,128)} fusion(bf16[16,2560]{1,0:T(8,128)(2,1)S(1)} %copy-done.4, bf16[16,256]{1,0:T(8,128)(2,1)} %param.24, f32[256]{0:T(256)} %param.25), kind=kOutput, calls=%fused_computation.6 | convolution fusion | flops 21626880 | bytes 2712576 | tf_op jit(solution)/shard_map/dot_general | solution.py:55
  87.6 1.8 %gather_fusion.2 = bf16[20,128,256]{2,1,0:T(8,128)(2,1)} fusion(bf16[16,128,256]{2,1,0:T(8,128)(2,1)S(1)} %bitcast.34, s32[1024]{0:T(1024)S(1)} %pad_clamp_fusion.1), kind=kCustom, calls=%fused_computation.2 | custom fusion | bytes 2621520 | tf_op jit(solution)/shard_map/gather | solution.py:35
  89.4 3.2 %gather_fusion = bf16[20,128,256]{2,1,0:T(8,128)(2,1)S(1)} fusion(bf16[80,128,256]{2,1,0:T(8,128)(2,1)} %bitcast.36, s32[1024]{0:T(1024)} %pad_clamp_fusion.2), kind=kCustom, calls=%fused_computation | custom fusion | bytes 2621520 | tf_op jit(solution)/shard_map/gather | solution.py:28
  92.6 0.0 copy-start.2
  92.7 1.7 %fusion.52 = f32[20,256,128]{1,2,0:T(8,128)S(1)} fusion(bf16[20,128,256]{2,1,0:T(8,128)(2,1)S(1)} %gather_fusion, bf16[20,2,128,128]{3,2,1,0:T(8,128)(2,1)} %param.16), kind=kOutput, calls=%fused_computation.66 | convolution fusion | flops 167772160 | bytes 4587520 | tf_op jit(solution)/shard_map/tij,tjc->tic/dot_general | solution.py:43
  94.4 0.1 copy-done.3
  94.5 0.5 convolution_add_fusion.3
  95.1 0.5 fusion.1
  95.6 0.2 copy-done.8
  95.7 9.7 %fusion.2 = bf16[2560,256]{1,0:T(8,128)(2,1)} fusion(bf16[256,256]{1,0:T(8,128)(2,1)S(1)} %all_gather.11, bf16[2560,256]{1,0:T(8,128)(2,1)S(1)} %copy-done.1, f32[256]{0:T(256)S(1)} %copy-done.8, f32[2560,256]{1,0:T(8,128)} %convolution_add_fusion.2, bf16[512,256]{1,0:T(8,128)(2,1)} %all_gather.10, bf16[2560,256]{1,0:T(8,128)(2,1)S(1)} %fusion.1), kind=kOutput, calls=%fused_computation.11 | convolution fusion | flops 1057751040 | bytes 6947840 | tf_op jit(solution)/shard_map/dot_general | solution.py:66
  (24 shorter events, 0.1 us)
Async XLA Ops:
  6.5 88.5 %copy-start = (bf16[2560,128]{1,0:T(8,128)(2,1)S(1)}, bf16[2560,128]{1,0:T(8,128)(2,1)}, u32[]{:S(2)}) copy-start(bf16[2560,128]{1,0:T(8,128)(2,1)} %param.17) | copy-start | bytes 1966084
  6.5 1.4 %copy-start.1 = (bf16[2560,256]{1,0:T(8,128)(2,1)S(1)}, bf16[2560,256]{1,0:T(8,128)(2,1)}, u32[]{:S(2)}) copy-start(bf16[2560,256]{1,0:T(8,128)(2,1)} %param.14) | copy-start | bytes 3932164
  6.5 82.8 %all-gather.2.cloned.1.call-start = ((), (), s32[]{:S(2)}) async-start(), calls=%async_computation.1 | async-start | bytes 6553600 | tf_op jit(solution)/shard_map/all_gather | solution.py:27
  8.0 7.5 %copy-start.6 = (s32[8]{0:T(128)S(1)}, s32[8]{0:T(128)}, u32[]{:S(2)}) copy-start(s32[8]{0:T(128)} %param.21) | copy-start | bytes 100
  15.5 8.6 %copy-start.7 = (s32[128]{0:T(128)S(1)}, s32[128]{0:T(128)}, u32[]{:S(2)}) copy-start(s32[128]{0:T(128)} %param.22) | copy-start | bytes 1540
  15.6 60.8 %copy-start.5 = (bf16[128,256]{1,0:T(8,128)(2,1)S(1)}, bf16[128,256]{1,0:T(8,128)(2,1)}, u32[]{:S(2)}) copy-start(bf16[128,256]{1,0:T(8,128)(2,1)} %param.23) | copy-start | bytes 196612
  15.6 69.3 %copy-start.4 = (bf16[16,2560]{1,0:T(8,128)(2,1)S(1)}, bf16[16,2560]{1,0:T(8,128)(2,1)}, u32[]{:S(2)}) copy-start(bf16[16,2560]{1,0:T(8,128)(2,1)} %param.15) | copy-start | bytes 245764
  16.8 70.8 %all-to-all-start = ((bf16[8,256,256]{2,1,0:T(8,128)(2,1)}), bf16[8,256,256]{2,1,0:T(8,128)(2,1)S(1)}, u32[]{:S(2)}, u32[]{:S(2)}) async-start(bf16[8,256,256]{2,1,0:T(8,128)(2,1)} %broadcast_select_fusion), calls=%async_computation | async-start | bytes 2097152 | tf_op jit(solution)/shard_map/all_to_all | solution.py:34
  92.6 1.8 %copy-start.2 = (bf16[20,128,256]{2,1,0:T(8,128)(2,1)S(1)}, bf16[20,128,256]{2,1,0:T(8,128)(2,1)}, u32[]{:S(2)}) copy-start(bf16[20,128,256]{2,1,0:T(8,128)(2,1)} %gather_fusion.2) | copy-start | bytes 3932164
  92.6 1.9 %copy-start.3 = (bf16[20,2,128,128]{3,2,1,0:T(8,128)(2,1)S(1)}, bf16[20,2,128,128]{3,2,1,0:T(8,128)(2,1)}, u32[]{:S(2)}) copy-start(bf16[20,2,128,128]{3,2,1,0:T(8,128)(2,1)} %param.16) | copy-start | bytes 3932164
  95.0 0.7 copy-start.8
Sparse Core Ops, SparseCore 0:
  8.9 43.8 all-gather.1
where the time goes:
time: 113 us; the launch traced here: 112 us
  blocking collectives  57.9 us (51%)
  matrix products  15.1 us (13%)
  local copies, waits for them, and re-layouts  13.7 us (12%)
  between operations  13.5 us (12%)
  starting transfers between devices  7.28 us (6%)
  other arithmetic  4.02 us (4%)
    psum x1, blocking collectives, per_device(): drivers = lax.psum(mine, ('dom', 'scen')).astype(jnp.bfloat16)  45.3 us
    dot_general x1, matrix products, per_device(): jnp.dot(columns, lax.all_gather(second_weight, 'scen', axis=0, tiled=True...  9.68 us
    gather x1, local copies, waits for them, and re-layouts, per_device(): embedding[send_rows]  7.5 us
    all_to_all x1, starting transfers between devices, per_device(): lax.all_to_all(outgoing_rows, 'dom', split_axis=0, concat_axis=0, tiled=T...  7.28 us
    all_gather x1, blocking collectives, per_device(): lax.all_gather(first_weight, 'scen', axis=0, tiled=True)  6.57 us
    all_gather x1, blocking collectives, per_device(): lax.all_gather(second_weight, 'scen', axis=0, tiled=True)  6.02 us
    gather x1, local copies, waits for them, and re-layouts, per_device(): local_tiles = partition.reshape(groups * tiles, tile, width)[local_slot]  3.24 us
    dot_general x1, matrix products, per_device(): jnp.dot(scenario_feats.T, feature_weight, preferred_element_type=jnp.floa...  2.72 us
  transfers between devices with their start and end apart: 2, of which 0 were waited for; matrix products, arithmetic and copies ran while one was open for 15% of the time, Pallas kernels for 0%

commit v1 on v0

v1 whole, which is shorter than its diff:
```python
import functools

import jax
import jax.numpy as jnp
from jax import lax
from jax.experimental import pallas as pl
from jax.experimental.pallas import tpu as pltpu
from jax.sharding import PartitionSpec as P

MESH = pl.DeviceIdType.MESH
LANES = 128
GROUP = 256
PAD = 16


def flipped(index, mask):
    bit = 1
    while bit <= mask:
        if mask & bit:
            index = index + bit * (1 - 2 * ((index // bit) % 2))
        bit *= 2
    return index


def spread(row):
    across = jnp.broadcast_to(row.astype(jnp.float32), (LANES, LANES))
    return across, across.T


def whole_part(values, size):
    return jnp.floor((values + 0.5) * (1.0 / size))


def iota_f32(shape, dim):
    return lax.broadcasted_iota(jnp.int32, shape, dim).astype(jnp.float32)


def picked_rows(column, emb_ref):
    tiles, tile, width = emb_ref.shape
    rows = tiles * tile
    lane = iota_f32(column.shape, 1)
    blocks = [
        jnp.where(column == lane + float(at), 1.0, 0.0).astype(jnp.bfloat16)
        for at in range(0, rows, LANES)
    ]
    return jnp.dot(
        jnp.concatenate(blocks, axis=1),
        emb_ref[...].reshape(rows, width),
        preferred_element_type=jnp.float32,
    ).astype(jnp.bfloat16)


def exchange_kernel(
    n_dom,
    n_scen,
    hot_ref,
    slot_ref,
    rows_ref,
    count_ref,
    emb_ref,
    w1_ref,
    w2_ref,
    halo_ref,
    local_ref,
    drv_ref,
    w1f_ref,
    w2f_ref,
    keys_ref,
    out_buf,
    stage,
    myreq,
    reqs,
    reqs_smem,
    mine,
    gat1,
    gat2,
    padrow,
    halo_send,
    halo_recv,
    req_send,
    req_recv,
    loc_send,
    loc_recv,
    d1_send,
    d1_recv,
    d2_send,
    d2_recv,
    w1_send,
    w1_recv,
    w2_send,
    w2_recv,
    own_sem,
):
    d = lax.axis_index("dom")
    s = lax.axis_index("scen")
    tiles, tile, _ = emb_ref.shape
    rows = tiles * tile
    per = tiles // n_scen
    cap = halo_ref.shape[0] // n_dom
    per_group = max(1, GROUP // cap)
    n_groups = n_dom // per_group
    drv_rows = n_dom * PAD

    def dom_peers(body):
        def step(k, carry):
            body(lax.rem(d + k, n_dom))
            return carry

        lax.fori_loop(1, n_dom, step, 0)

    def scen_peers(body):
        for k in range(n_scen - 1, 0, -1):
            body(flipped(s, k))

    def remote(src, dst, send, recv, where):
        return pltpu.make_async_remote_copy(
            src_ref=src,
            dst_ref=dst,
            send_sem=send,
            recv_sem=recv,
            device_id=where,
            device_id_type=MESH,
        )

    def block(ref, index, size):
        return ref.at[pl.ds(pl.multiple_of(index * size, size), size)]

    def halo_copy(peer, mark):
        return remote(
            block(out_buf, peer, cap),
            block(halo_ref, mark, cap),
            halo_send.at[peer],
            halo_recv.at[mark],
            {"dom": peer},
        )

    def req_copy(peer, mark):
        return remote(myreq, reqs.at[mark], req_send.at[peer], req_recv.at[mark], {"scen": peer})

    def loc_copy(peer, mark):
        return remote(
            block(stage, peer, per * tile),
            block(local_ref, mark, per * tile),
            loc_send.at[peer],
            loc_recv.at[mark],
            {"scen": peer},
        )

    def d1_copy(peer, mark):
        return remote(
            mine, block(gat1, mark, PAD), d1_send.at[peer], d1_recv.at[mark], {"dom": peer}
        )

    def d2_copy(peer, mark):
        return remote(
            gat1, block(gat2, mark, drv_rows), d2_send.at[peer], d2_recv.at[mark], {"scen": peer}
        )

    def w1_copy(peer, mark):
        return remote(
            w1_ref,
            block(w1f_ref, mark, w1_ref.shape[0]),
            w1_send.at[peer],
            w1_recv.at[mark],
            {"scen": peer},
        )

    def w2_copy(peer, mark):
        return remote(
            w2_ref,
            block(w2f_ref, mark, w2_ref.shape[0]),
            w2_send.at[peer],
            w2_recv.at[mark],
            {"scen": peer},
        )

    barrier = pltpu.get_barrier_semaphore()
    dom_peers(
        lambda p: pl.semaphore_signal(
            barrier, inc=1, device_id={"dom": p}, device_id_type=MESH
        )
    )
    scen_peers(
        lambda u: pl.semaphore_signal(
            barrier, inc=1, device_id={"scen": u}, device_id_type=MESH
        )
    )

    square = (LANES, LANES)
    lane = iota_f32(square, 1)
    sub = iota_f32(square, 0)

    padrow[...] = jnp.full(padrow.shape, -1, jnp.int32)
    padrow[0:1, 0:tiles] = slot_ref[...]
    across = jnp.broadcast_to(padrow[0:1, :], square)
    down = across.T
    ilane = lax.broadcasted_iota(jnp.int32, square, 1)
    isub = lax.broadcasted_iota(jnp.int32, square, 0)

    def holder(slots):
        found = jnp.where(slots >= 0, 0, -1)
        for u in range(1, n_scen):
            found = found + jnp.where(slots >= u * tiles, 1, 0)
        return found

    own_a, own_d = holder(across), holder(down)
    same = own_a == own_d
    rank_col = jnp.sum(jnp.where(same & (ilane < isub), 1, 0), axis=1, keepdims=True)
    rank_row = jnp.sum(jnp.where(same & (isub < ilane), 1, 0), axis=0, keepdims=True)
    key_col = jnp.where(isub < tiles, own_d * per + rank_col, -1)
    wanted = jnp.sum(
        jnp.where(key_col == ilane, down - own_d * tiles, 0), axis=0, keepdims=True
    )
    myreq[...] = jnp.broadcast_to(wanted, myreq.shape)
    keys_ref[...] = jnp.broadcast_to(own_a[0:1, :] * per + rank_row, keys_ref.shape)

    pl.semaphore_wait(barrier, n_dom - 1 + n_scen - 1)
    scen_peers(lambda u: req_copy(u, s).start())

    def row_of(index, columns):
        block_of = rows_ref[:, columns]
        at = lax.broadcasted_iota(jnp.int32, block_of.shape, 0)
        return jnp.sum(jnp.where(at == index, block_of, 0), axis=0, keepdims=True)

    def halo_group(group):
        first = group * per_group
        columns = []
        for half in range(GROUP // LANES):
            if cap >= LANES:
                parts = cap // LANES
                assert per_group == 1 and parts == GROUP // LANES
                row = row_of(first, slice(half * LANES, (half + 1) * LANES))
                limit = count_ref[first]
                place = lax.broadcasted_iota(jnp.int32, (1, LANES), 1) + half * LANES
                row = jnp.where(place < limit, row, -1)
            else:
                parts = LANES // cap
                row = row_of(group * (GROUP // LANES) + half, slice(0, LANES))
                place = lax.broadcasted_iota(jnp.int32, (1, LANES), 1)
                live = place < 0
                for i in range(parts):
                    limit = count_ref[first + half * parts + i]
                    live = live | ((place >= i * cap) & (place < i * cap + limit) & (place < (i + 1) * cap))
                row = jnp.where(live, row, -1)
            columns.append(spread(row)[1])
        block(out_buf, group, GROUP)[...] = picked_rows(
            jnp.concatenate(columns, axis=0), emb_ref
        )

    def halo_start(group):
        halo_group(group)
        if per_group == 1:
            halo_copy(group, d).start()
            return

        def step(i, carry):
            p = group * per_group + i

            @pl.when(p != d)
            def _():
                halo_copy(p, d).start()

            return carry

        lax.fori_loop(0, per_group, step, 0)

    my_group = d // per_group
    order = list(range(n_groups - 1, 0, -1))
    halo_start(flipped(my_group, order[0]))

    r_ids, c_ids = spread(hot_ref[...])
    r_own, c_own = whole_part(r_ids, rows), whole_part(c_ids, rows)
    equal = r_ids == c_ids
    new_col = 1.0 - jnp.max(jnp.where(equal & (lane < sub), 1.0, 0.0), axis=1, keepdims=True)
    new_row = 1.0 - jnp.max(jnp.where(equal & (sub < lane), 1.0, 0.0), axis=0, keepdims=True)
    alike = r_own == c_own
    hot_rank_row = jnp.sum(
        jnp.where(alike & (c_ids < r_ids), new_col, 0.0), axis=0, keepdims=True
    )
    hot_rank_col = jnp.sum(
        jnp.where(alike & (r_ids < c_ids), new_row, 0.0), axis=1, keepdims=True
    )
    me = (d * n_scen + s).astype(jnp.float32)
    own_rows = picked_rows(c_ids - me * float(rows), emb_ref)
    chosen = jnp.where(
        (iota_f32((PAD, LANES), 0) == hot_rank_row) & (r_own[0:1, :] == me), new_row, 0.0
    ).astype(jnp.bfloat16)
    mine[...] = jnp.dot(chosen, own_rows, preferred_element_type=jnp.float32).astype(jnp.bfloat16)
    block(gat1, d, PAD)[...] = mine[...]
    dom_peers(lambda p: d1_copy(p, d).start())

    halo_start(flipped(my_group, order[1]))

    scen_peers(lambda u: req_copy(u, u).wait_recv())
    reqs[pl.ds(s, 1)] = myreq[...][None]
    fetch = pltpu.make_async_copy(reqs, reqs_smem, own_sem.at[0])
    fetch.start()
    fetch.wait()

    def stage_for(u):
        for r in range(per):
            slot = reqs_smem[u, 0, s * per + r]
            block(stage, u * per + r, tile)[...] = emb_ref[slot]

    def serve(u):
        stage_for(u)
        loc_copy(u, s).start()

    scen_peers(serve)
    scen_peers(lambda u: w1_copy(u, s).start())
    scen_peers(lambda u: w2_copy(u, s).start())
    stage_for(s)
    own_copies = [
        pltpu.make_async_copy(
            block(stage, s, per * tile), block(local_ref, s, per * tile), own_sem.at[0]
        ),
        pltpu.make_async_copy(w1_ref, block(w1f_ref, s, w1_ref.shape[0]), own_sem.at[1]),
        pltpu.make_async_copy(w2_ref, block(w2f_ref, s, w2_ref.shape[0]), own_sem.at[2]),
    ]
    for copy in own_copies:
        copy.start()

    for mask in order[2:]:
        halo_start(flipped(my_group, mask))
    if per_group == 1:
        halo_group(my_group)
    else:
        halo_start(my_group)
    own_halo = pltpu.make_async_copy(
        block(out_buf, d, cap), block(halo_ref, d, cap), own_sem.at[3]
    )
    own_halo.start()

    dom_peers(lambda p: d1_copy(p, p).wait_recv())
    scen_peers(lambda u: d2_copy(u, s).start())
    block(gat2, s, drv_rows)[...] = gat1[...]
    scen_peers(lambda u: d2_copy(u, u).wait_recv())
    c_dom = whole_part(c_own, n_scen)
    place = (c_own - c_dom * float(n_scen)) * float(drv_rows) + c_dom * float(PAD) + hot_rank_col
    total = jnp.zeros(drv_ref.shape, jnp.float32)
    for at in range(0, n_scen * drv_rows, LANES):
        pick = jnp.where(place == lane + float(at), 1.0, 0.0).astype(jnp.bfloat16)
        total += jnp.dot(pick, gat2[at : at + LANES, :], preferred_element_type=jnp.float32)
    drv_ref[...] = total.astype(jnp.bfloat16)

    for copy in own_copies:
        copy.wait()
    own_halo.wait()
    dom_peers(lambda p: d1_copy(p, p).wait_send())
    for make in (req_copy, d2_copy):
        scen_peers(lambda u: make(u, u).wait_send())
    for make in (w1_copy, w2_copy, loc_copy):
        scen_peers(lambda u: make(u, u).wait())
    dom_peers(lambda p: halo_copy(p, p).wait())


def exchange(hot_ids, local_slot, send_rows, send_count, embedding, w1, w2, n_dom, n_scen, tile):
    rows, width = embedding.shape
    slots = send_rows.size
    cap = send_rows.shape[1]
    hot = hot_ids.shape[0]
    assert -(-hot // (n_dom * n_scen)) <= PAD
    if cap < LANES:
        send_rows = send_rows.reshape(-1, LANES)
    vmem = pl.BlockSpec(memory_space=pltpu.VMEM)
    smem = pl.BlockSpec(memory_space=pltpu.SMEM)
    anywhere = pl.BlockSpec(memory_space=pl.ANY)
    bf16 = jnp.bfloat16
    dma = pltpu.SemaphoreType.DMA
    return pl.pallas_call(
        functools.partial(exchange_kernel, n_dom, n_scen),
        out_shape=(
            jax.ShapeDtypeStruct((slots, width), bf16),
            jax.ShapeDtypeStruct((rows, width), bf16),
            jax.ShapeDtypeStruct((hot, width), bf16),
            jax.ShapeDtypeStruct((n_scen * w1.shape[0], width), bf16),
            jax.ShapeDtypeStruct((n_scen * w2.shape[0], width), bf16),
            jax.ShapeDtypeStruct((8, LANES), jnp.int32),
        ),
        in_specs=[vmem, vmem, vmem, smem, vmem, anywhere, anywhere],
        out_specs=(anywhere, anywhere, vmem, anywhere, anywhere, vmem),
        scratch_shapes=[
            pltpu.VMEM((slots, width), bf16),
            pltpu.VMEM((rows, width), bf16),
            pltpu.VMEM((8, LANES), jnp.int32),
            pltpu.VMEM((n_scen, 8, LANES), jnp.int32),
            pltpu.SMEM((n_scen, 8, LANES), jnp.int32),
            pltpu.VMEM((PAD, width), bf16),
            pltpu.VMEM((n_dom * PAD, width), bf16),
            pltpu.VMEM((n_scen * n_dom * PAD, width), bf16),
            pltpu.VMEM((8, LANES), jnp.int32),
            dma((n_dom,)),
            dma((n_dom,)),
            dma((n_scen,)),
            dma((n_scen,)),
            dma((n_scen,)),
            dma((n_scen,)),
            dma((n_dom,)),
            dma((n_dom,)),
            dma((n_scen,)),
            dma((n_scen,)),
            dma((n_scen,)),
            dma((n_scen,)),
            dma((n_scen,)),
            dma((n_scen,)),
            dma((4,)),
        ],
        compiler_params=pltpu.CompilerParams(
            collective_id=0, has_side_effects=True, vmem_limit_bytes=40 * 1024 * 1024
        ),
        name="exchange",
    )(
        hot_ids.reshape(1, -1),
        local_slot.reshape(1, -1),
        send_rows,
        send_count,
        embedding.reshape(-1, tile, width),
        w1,
        w2,
    )


def update_kernel(
    count,
    keys_ref,
    halo_slot_ref,
    emb_ref,
    feats_ref,
    adj_ref,
    dw_ref,
    halo_ref,
    local_ref,
    drv_ref,
    w1_ref,
    fw_ref,
    b1_ref,
    w2_ref,
    b2_ref,
    out_ref,
    agg_ref,
):
    step = pl.program_id(0)
    tile = adj_ref.shape[-1]
    width = emb_ref.shape[1]
    for i in range(count):
        key = keys_ref[0, step * count + i]
        slot = halo_slot_ref[step * count + i]
        local = local_ref[pl.ds(pl.multiple_of(key * tile, tile), tile), :]
        halo = halo_ref[pl.ds(pl.multiple_of(slot * tile, tile), tile), :]
        here = slice(i * tile, (i + 1) * tile)
        total = jnp.dot(adj_ref[i, 0], local, preferred_element_type=jnp.float32)
        total += jnp.dot(adj_ref[i, 1], halo, preferred_element_type=jnp.float32)
        total += jnp.dot(dw_ref[here, :], drv_ref[...], preferred_element_type=jnp.float32)
        agg_ref[here, :] = total.astype(jnp.bfloat16)
    emb = emb_ref[...]
    inner = jnp.dot(emb, w1_ref[:width, :], preferred_element_type=jnp.float32)
    inner += jnp.dot(agg_ref[...], w1_ref[width:, :], preferred_element_type=jnp.float32)
    inner += lax.dot_general(
        feats_ref[...],
        fw_ref[...],
        (((0,), (0,)), ((), ())),
        preferred_element_type=jnp.float32,
    )
    inner += b1_ref[...]
    activated = (0.5 * inner * (1.0 + lax.erf(inner * (0.5**0.5)))).astype(jnp.bfloat16)
    result = jnp.dot(activated, w2_ref[...], preferred_element_type=jnp.float32)
    out_ref[...] = (result + (emb.astype(jnp.float32) + b2_ref[...])).astype(jnp.bfloat16)


def update(keys, halo_slot, embedding, feats, adjacency, dw, halo, local, drv, w1, fw, b1, w2, b2):
    rows, width = embedding.shape
    tiles, _, tile, _ = adjacency.shape
    count = 4 if tiles % 4 == 0 else 1
    part = count * tile

    def all_of(array):
        return pl.BlockSpec(array.shape, lambda i, *_: (0,) * array.ndim)

    b1, b2 = b1.reshape(1, -1), b2.reshape(1, -1)
    grid_spec = pltpu.PrefetchScalarGridSpec(
        num_scalar_prefetch=2,
        grid=(tiles // count,),
        in_specs=[
            pl.BlockSpec((part, width), lambda i, *_: (i, 0)),
            pl.BlockSpec((feats.shape[0], part), lambda i, *_: (0, i)),
            pl.BlockSpec((count, 2, tile, tile), lambda i, *_: (i, 0, 0, 0)),
            pl.BlockSpec((part, dw.shape[1]), lambda i, *_: (i, 0)),
            all_of(halo),
            all_of(local),
            all_of(drv),
            all_of(w1),
            all_of(fw),
            all_of(b1),
            all_of(w2),
            all_of(b2),
        ],
        out_specs=pl.BlockSpec((part, width), lambda i, *_: (i, 0)),
        scratch_shapes=[pltpu.VMEM((part, width), jnp.bfloat16)],
    )
    return pl.pallas_call(
        functools.partial(update_kernel, count),
        grid_spec=grid_spec,
        out_shape=jax.ShapeDtypeStruct((rows, width), jnp.bfloat16),
        compiler_params=pltpu.CompilerParams(vmem_limit_bytes=40 * 1024 * 1024),
        name="update",
    )(keys, halo_slot, embedding, feats, adjacency, dw, halo, local, drv, w1, fw, b1, w2, b2)


def per_device(
    embedding,
    scenario_feats,
    adjacency,
    driver_weight,
    local_slot,
    halo_slot,
    send_rows,
    send_count,
    hot_ids,
    first_weight,
    feature_weight,
    first_bias,
    second_weight,
    second_bias,
):
    n_dom, n_scen = lax.axis_size("dom"), lax.axis_size("scen")
    halo, local, drivers, w1, w2, keys = exchange(
        hot_ids,
        local_slot,
        send_rows,
        send_count,
        embedding,
        first_weight,
        second_weight,
        n_dom,
        n_scen,
        adjacency.shape[-1],
    )
    return update(
        keys,
        halo_slot,
        embedding,
        scenario_feats,
        adjacency,
        driver_weight,
        halo,
        local,
        drivers,
        w1,
        feature_weight,
        first_bias,
        w2,
        second_bias,
    )


def solution(mesh):
    return jax.shard_map(
        per_device,
        mesh=mesh,
        in_specs=(
            P(("dom", "scen"), None),
            P(None, ("dom", "scen")),
            P(("dom", "scen"), None, None, None),
            P(("dom", "scen"), None),
            P(("dom", "scen")),
            P(("dom", "scen")),
            P(("dom", "scen"), None),
            P(("dom", "scen")),
            P(),
            P("scen", None),
            P(),
            P(),
            P("scen", None),
            P(),
        ),
        out_specs=P(("dom", "scen"), None),
        check_vma=False,
    )
```

time: 113 us -> 47.7 us (0.42)
  blocking collectives: 57.9 us -> 0 us
  Pallas kernels: 0 us -> 39.2 us
  matrix products: 15.1 us -> 0 us
  between operations: 13.5 us -> 0.08 us
  starting transfers between devices: 7.28 us -> 0 us
  local copies, waits for them, and re-layouts: 13.7 us -> 8.02 us
  other arithmetic: 4.02 us -> 0 us
    psum x1 -> x0, blocking collectives: 45.3 us -> none  [per_device(): drivers = lax.psum(mine, ('dom', 'scen')).astype(jnp.bfloat16)]
    pallas_call x0 -> x2, Pallas kernels: none -> 39.2 us  [the longest x1 33.9 us: exchange(): pl.pallas_call(functools.partial(exchange_kernel, n_dom, n_scen), out_sha...]
    dot_general x5 -> x0, matrix products: 15.1 us -> none  [the longest x1 9.68 us: per_device(): jnp.dot(columns, lax.all_gather(second_weight, 'scen', axis=0, tiled=True...]
    gather x4 -> x0, local copies, waits for them, and re-layouts: 13.3 us -> none  [the longest x1 7.5 us: per_device(): embedding[send_rows]]
    all_gather x2 -> x0, blocking collectives: 12.6 us -> none  [the longest x1 6.57 us: per_device(): lax.all_gather(first_weight, 'scen', axis=0, tiled=True)]
    unnamed x19 -> x30, local copies, waits for them, and re-layouts: 0.36 us -> 8.02 us
    all_to_all x1 -> x0, starting transfers between devices: 7.28 us -> none  [per_device(): lax.all_to_all(outgoing_rows, 'dom', split_axis=0, concat_axis=0, tiled=T...]
    select_n x5 -> x0, other arithmetic: 2.62 us -> none  [the longest x1 1.21 us: per_device(): jnp.where(live[:, :, None], embedding[send_rows], jnp.zeros((), embedding...]
  transfers between devices with their start and end apart: 2 -> 0, of which waited for: 0 -> 0; matrix products, arithmetic and copies ran while one was open for 15% -> 0% of each run, Pallas kernels for 0% -> 0%
where the time goes in v1:
time: 47.7 us; the launch traced here: 47.3 us
  Pallas kernels  39.2 us (82%)
  local copies, waits for them, and re-layouts  8.02 us (17%)
    pallas_call x1, Pallas kernels, exchange(): pl.pallas_call(functools.partial(exchange_kernel, n_dom, n_scen), out_sha...  33.9 us
    unnamed x30, local copies, waits for them, and re-layouts  8.02 us
    pallas_call x1, Pallas kernels, update(): pl.pallas_call(functools.partial(update_kernel, count), grid_spec=grid_sp...  5.28 us

profile of v1, /device:TPU:0, one launch (start us, length us, event | category | flops | bytes accessed | tf_op | source)
XLA Modules:
  0.0 47.3 jit_solution(5540256172783752663)
XLA Ops:
  0.0 0.0 copy-start.9
  0.0 0.0 copy-start.8
  0.0 0.0 copy-start
  0.0 1.3 %copy-done = bf16[2560,256]{1,0:T(8,128)(2,1)S(1)} copy-done((bf16[2560,256]{1,0:T(8,128)(2,1)S(1)}, bf16[2560,256]{1,0:T(8,128)(2,1)}, u32[]{:S(2)}) %copy-start) | copy-done | bytes 1310744
  1.4 0.8 %copy-done.5 = bf16[128,256]{1,0:T(8,128)(2,1)S(1)} copy-done((bf16[128,256]{1,0:T(8,128)(2,1)S(1)}, bf16[128,256]{1,0:T(8,128)(2,1)}, u32[]{:S(2)}) %copy-start.5) | copy-done | bytes 65560
  2.2 0.8 %copy-done.6 = bf16[64,256]{1,0:T(8,128)(2,1)S(1)} copy-done((bf16[64,256]{1,0:T(8,128)(2,1)S(1)}, bf16[64,256]{1,0:T(8,128)(2,1)}, u32[]{:S(2)}) %copy-start.6) | copy-done | bytes 32792
  2.9 0.0 copy-start.7
  2.9 0.7 %copy-done.7 = s32[8,256]{1,0:T(8,128)S(1)} copy-done((s32[8,256]{1,0:T(8,128)S(1)}, s32[8,256]{1,0:T(8,128)}, u32[]{:S(2)}) %copy-start.7) | copy-done | bytes 8216
  3.6 0.0 copy-start.11
  3.6 0.7 %copy-done.11 = s32[128]{0:T(128)S(1)} copy-done((s32[128]{0:T(128)S(1)}, s32[128]{0:T(128)}, u32[]{:S(2)}) %copy-start.11) | copy-done | bytes 536
  4.3 0.0 copy-start.12
  4.3 0.7 %copy-done.12 = s32[20]{0:T(128)S(1)} copy-done((s32[20]{0:T(128)S(1)}, s32[20]{0:T(128)}, u32[]{:S(2)}) %copy-start.12) | copy-done | bytes 104
  5.0 0.7 %copy-done.13 = s32[8]{0:T(128)S(1)} copy-done((s32[8]{0:T(128)S(1)}, s32[8]{0:T(128)}, u32[]{:S(2)}) %copy-start.13) | copy-done | bytes 56
  5.6 33.9 %exchange.1 = (bf16[2048,256]{1,0:T(8,128)(2,1)S(1)}, bf16[2560,256]{1,0:T(8,128)(2,1)S(1)}, bf16[128,256]{1,0:T(8,128)(2,1)S(1)}, bf16[512,256]{1,0:T(8,128)(2,...) custom-call(s32[1,128]{1,0:T(1,128)S(1)} %bitcast.8, s32[1,20]{1,0:T(1,128)S(1)} %bitcast.9, ...), custom_call_target="tpu_custom_call" | custom-call | tf_op jit(solution)/shard_map/exchange/pallas_call | solution.py:370
  39.6 0.0 copy-done.9
  39.6 0.0 copy-done.8
  39.6 0.0 copy-done.1
  39.6 0.0 copy-done.4
  39.6 0.0 copy-done.10
  39.6 0.0 copy-done.14
  39.6 0.0 copy-start.2
  39.6 1.3 %copy-done.2 = bf16[20,2,128,128]{3,2,1,0:T(8,128)(2,1)S(1)} copy-done((bf16[20,2,128,128]{3,2,1,0:T(8,128)(2,1)S(1)}, bf16[20,2,128,128]{3,2,1,0:T(8,128)(2,1)}, u32[]{:S(2)}) %copy-start.2) | copy-done | bytes 1310744
  41.0 1.1 %copy-done.3 = bf16[2560,128]{1,0:T(8,128)(2,1)S(1)} copy-done((bf16[2560,128]{1,0:T(8,128)(2,1)S(1)}, bf16[2560,128]{1,0:T(8,128)(2,1)}, u32[]{:S(2)}) %copy-start.3) | copy-done | bytes 655384
  42.0 5.3 %update.1 = bf16[2560,256]{1,0:T(8,128)(2,1)} custom-call(s32[8,128]{1,0:T(8,128)S(1)} %get-tuple-element.11.keys_ref, s32[20]{0:T(128)S(1)} %copy-done.14, bf16[2560,256]{1,0:T(8,128)(2,1)S(1)} %copy-done.1, bf16[16,2560]{1,0:T(8,128)(2,1)S(1)} %copy-done.4, bf16[20,2,128,128]{3,2,1,0:T(8,128)(2,1)S(1)} %copy-done.2, bf16[2560,128]{1,0:T(8,128)(2,1)S(1)} %copy-done.3, ...), custom_call_target="tpu_custom_call" | custom-call | tf_op jit(solution)/shard_map/update/pallas_call | solution.py:500
  (8 shorter events, 0.0 us)
Async XLA Ops:
  0.0 39.6 %copy-start.9 = (f32[256]{0:T(256)S(1)}, f32[256]{0:T(256)}, u32[]{:S(2)}) copy-start(f32[256]{0:T(256)} %param.25) | copy-start | bytes 3076
  0.0 39.6 %copy-start.8 = (bf16[16,256]{1,0:T(8,128)(2,1)S(1)}, bf16[16,256]{1,0:T(8,128)(2,1)}, u32[]{:S(2)}) copy-start(bf16[16,256]{1,0:T(8,128)(2,1)} %fw_ref.1) | copy-start | bytes 24580
  0.0 1.3 %copy-start = (bf16[2560,256]{1,0:T(8,128)(2,1)S(1)}, bf16[2560,256]{1,0:T(8,128)(2,1)}, u32[]{:S(2)}) copy-start(bf16[2560,256]{1,0:T(8,128)(2,1)} %emb_ref.1) | copy-start | bytes 3932164
  1.3 0.8 %copy-start.5 = (bf16[128,256]{1,0:T(8,128)(2,1)S(1)}, bf16[128,256]{1,0:T(8,128)(2,1)}, u32[]{:S(2)}) copy-start(bf16[128,256]{1,0:T(8,128)(2,1)} %w1_ref.1) | copy-start | bytes 196612
  2.2 0.8 %copy-start.6 = (bf16[64,256]{1,0:T(8,128)(2,1)S(1)}, bf16[64,256]{1,0:T(8,128)(2,1)}, u32[]{:S(2)}) copy-start(bf16[64,256]{1,0:T(8,128)(2,1)} %w2_ref.1) | copy-start | bytes 98308
  2.9 0.7 %copy-start.7 = (s32[8,256]{1,0:T(8,128)S(1)}, s32[8,256]{1,0:T(8,128)}, u32[]{:S(2)}) copy-start(s32[8,256]{1,0:T(8,128)} %rows_ref.1) | copy-start | bytes 24580
  3.6 0.7 %copy-start.11 = (s32[128]{0:T(128)S(1)}, s32[128]{0:T(128)}, u32[]{:S(2)}) copy-start(s32[128]{0:T(128)} %param.22) | copy-start | bytes 1540
  4.3 0.7 %copy-start.12 = (s32[20]{0:T(128)S(1)}, s32[20]{0:T(128)}, u32[]{:S(2)}) copy-start(s32[20]{0:T(128)} %param.18) | copy-start | bytes 244
  5.0 0.7 %copy-start.13 = (s32[8]{0:T(128)S(1)}, s32[8]{0:T(128)}, u32[]{:S(2)}) copy-start(s32[8]{0:T(128)} %count_ref.1) | copy-start | bytes 100
  5.6 34.0 %copy-start.1 = (bf16[2560,256]{1,0:T(8,128)(2,1)S(1)}, bf16[2560,256]{1,0:T(8,128)(2,1)}, u32[]{:S(2)}) copy-start(bf16[2560,256]{1,0:T(8,128)(2,1)} %emb_ref.1) | copy-start | bytes 3932164
  5.6 34.0 %copy-start.4 = (bf16[16,2560]{1,0:T(8,128)(2,1)S(1)}, bf16[16,2560]{1,0:T(8,128)(2,1)}, u32[]{:S(2)}) copy-start(bf16[16,2560]{1,0:T(8,128)(2,1)} %feats_ref.1) | copy-start | bytes 245764
  5.6 34.0 %copy-start.10 = (f32[256]{0:T(256)S(1)}, f32[256]{0:T(256)}, u32[]{:S(2)}) copy-start(f32[256]{0:T(256)} %param.27) | copy-start | bytes 3076
  5.6 34.0 %copy-start.14 = (s32[20]{0:T(128)S(1)}, s32[20]{0:T(128)}, u32[]{:S(2)}) copy-start(s32[20]{0:T(128)} %halo_slot_ref.1) | copy-start | bytes 244
  39.6 1.3 %copy-start.2 = (bf16[20,2,128,128]{3,2,1,0:T(8,128)(2,1)S(1)}, bf16[20,2,128,128]{3,2,1,0:T(8,128)(2,1)}, u32[]{:S(2)}) copy-start(bf16[20,2,128,128]{3,2,1,0:T(8,128)(2,1)} %adj_ref.1) | copy-start | bytes 3932164
  41.0 1.1 %copy-start.3 = (bf16[2560,128]{1,0:T(8,128)(2,1)S(1)}, bf16[2560,128]{1,0:T(8,128)(2,1)}, u32[]{:S(2)}) copy-start(bf16[2560,128]{1,0:T(8,128)(2,1)} %dw_ref.1) | copy-start | bytes 1966084

commit v2 on v1

v2 whole, which is shorter than its diff:
```python
import functools

import jax
import jax.numpy as jnp
from jax import lax
from jax.experimental import pallas as pl
from jax.experimental.pallas import tpu as pltpu
from jax.sharding import PartitionSpec as P

MESH = pl.DeviceIdType.MESH
LANES = 128
GROUP = 256
PAD = 16


def flipped(index, mask):
    bit = 1
    while bit <= mask:
        if mask & bit:
            index = index + bit * (1 - 2 * ((index // bit) % 2))
        bit *= 2
    return index


def spread(row):
    across = jnp.broadcast_to(row.astype(jnp.float32), (LANES, LANES))
    return across, across.T


def whole_part(values, size):
    return jnp.floor((values + 0.5) * (1.0 / size))


def iota_f32(shape, dim):
    return lax.broadcasted_iota(jnp.int32, shape, dim).astype(jnp.float32)


def picked_rows(column, emb_ref):
    tiles, tile, width = emb_ref.shape
    rows = tiles * tile
    lane = iota_f32(column.shape, 1)
    blocks = [
        jnp.where(column == lane + float(at), 1.0, 0.0).astype(jnp.bfloat16)
        for at in range(0, rows, LANES)
    ]
    return jnp.dot(
        jnp.concatenate(blocks, axis=1),
        emb_ref[...].reshape(rows, width),
        preferred_element_type=jnp.float32,
    ).astype(jnp.bfloat16)


def layer_kernel(
    n_dom,
    n_scen,
    cap,
    hot_hbm,
    slot_hbm,
    halo_slot_hbm,
    rows_hbm,
    count_hbm,
    emb_hbm,
    feats_hbm,
    adj_hbm,
    dw_hbm,
    w1_hbm,
    fw_hbm,
    b1_hbm,
    w2_hbm,
    b2_hbm,
    result_hbm,
    hot_ref,
    slot_ref,
    halo_slot_ref,
    rows_ref,
    count_ref,
    emb_ref,
    feats_ref,
    adj_ref,
    dw_ref,
    fw_ref,
    b1_ref,
    b2_ref,
    w1f_ref,
    w2f_ref,
    halo_ref,
    local_ref,
    drv_ref,
    keys_ref,
    keys_smem,
    out_buf,
    stage,
    myreq,
    reqs,
    reqs_smem,
    mine,
    gat1,
    gat2,
    padrow,
    agg_ref,
    inner_ref,
    result_ref,
    in_sem,
    halo_send,
    halo_recv,
    req_send,
    req_recv,
    loc_send,
    loc_recv,
    d1_send,
    d1_recv,
    d2_send,
    d2_recv,
    w1_send,
    w1_recv,
    w2_send,
    w2_recv,
    own_sem,
    result_sem,
):
    d = lax.axis_index("dom")
    s = lax.axis_index("scen")
    tiles, tile, width = emb_ref.shape
    rows = tiles * tile
    per = tiles // n_scen
    per_group = max(1, GROUP // cap)
    n_groups = n_dom // per_group
    drv_rows = n_dom * PAD

    def dom_peers(body):
        def step(k, carry):
            body(lax.rem(d + k, n_dom))
            return carry

        lax.fori_loop(1, n_dom, step, 0)

    def scen_peers(body):
        for k in range(n_scen - 1, 0, -1):
            body(flipped(s, k))

    def remote(src, dst, send, recv, where):
        return pltpu.make_async_remote_copy(
            src_ref=src,
            dst_ref=dst,
            send_sem=send,
            recv_sem=recv,
            device_id=where,
            device_id_type=MESH,
        )

    def block(ref, index, size):
        return ref.at[pl.ds(pl.multiple_of(index * size, size), size)]

    def halo_place(index):
        if cap >= tile:
            return halo_ref.at[pl.ds(index * (cap // tile), cap // tile)]
        share = tile // cap
        return halo_ref.at[
            index // share, pl.ds(pl.multiple_of((index % share) * cap, cap), cap)
        ]

    def halo_source(index):
        if cap >= tile:
            return out_buf.at[pl.ds(index * (cap // tile), cap // tile)]
        share = tile // cap
        return out_buf.at[
            index // share, pl.ds(pl.multiple_of((index % share) * cap, cap), cap)
        ]

    def halo_copy(peer, mark):
        return remote(
            halo_source(peer),
            halo_place(mark),
            halo_send.at[peer],
            halo_recv.at[mark],
            {"dom": peer},
        )

    def req_copy(peer, mark):
        return remote(myreq, reqs.at[mark], req_send.at[peer], req_recv.at[mark], {"scen": peer})

    def loc_copy(peer, mark):
        return remote(
            stage.at[pl.ds(peer * per, per)],
            local_ref.at[pl.ds(mark * per, per)],
            loc_send.at[peer],
            loc_recv.at[mark],
            {"scen": peer},
        )

    def d1_copy(peer, mark):
        return remote(
            mine, block(gat1, mark, PAD), d1_send.at[peer], d1_recv.at[mark], {"dom": peer}
        )

    def d2_copy(peer, mark):
        return remote(
            gat1, block(gat2, mark, drv_rows), d2_send.at[peer], d2_recv.at[mark], {"scen": peer}
        )

    def w1_copy(peer, mark):
        return remote(
            w1_hbm,
            block(w1f_ref, mark, w1_hbm.shape[0]),
            w1_send.at[peer],
            w1_recv.at[mark],
            {"scen": peer},
        )

    def w2_copy(peer, mark):
        return remote(
            w2_hbm,
            block(w2f_ref, mark, w2_hbm.shape[0]),
            w2_send.at[peer],
            w2_recv.at[mark],
            {"scen": peer},
        )

    loads = {}

    def load(name, src, dst):
        loads[name] = pltpu.make_async_copy(src, dst, in_sem.at[len(loads)])
        loads[name].start()

    load("slot", slot_hbm, slot_ref)
    load("count", count_hbm, count_ref)
    load("rows", rows_hbm, rows_ref)
    load("hot", hot_hbm, hot_ref)
    load("emb", emb_hbm, emb_ref)

    barrier = pltpu.get_barrier_semaphore()
    dom_peers(
        lambda p: pl.semaphore_signal(
            barrier, inc=1, device_id={"dom": p}, device_id_type=MESH
        )
    )
    scen_peers(
        lambda u: pl.semaphore_signal(
            barrier, inc=1, device_id={"scen": u}, device_id_type=MESH
        )
    )

    load("halo_slot", halo_slot_hbm, halo_slot_ref)
    load("w1", w1_hbm, block(w1f_ref, s, w1_hbm.shape[0]))
    load("w2", w2_hbm, block(w2f_ref, s, w2_hbm.shape[0]))
    load("feats", feats_hbm, feats_ref)
    load("fw", fw_hbm, fw_ref)
    load("b1", b1_hbm, b1_ref)
    load("b2", b2_hbm, b2_ref)
    load("dw", dw_hbm, dw_ref)
    load("adj", adj_hbm, adj_ref)

    square = (LANES, LANES)
    lane = iota_f32(square, 1)
    sub = iota_f32(square, 0)

    padrow[...] = jnp.full(padrow.shape, -1, jnp.int32)
    loads["slot"].wait()
    padrow[0:1, 0:tiles] = slot_ref[...]
    across = jnp.broadcast_to(padrow[0:1, :], square)
    down = across.T
    ilane = lax.broadcasted_iota(jnp.int32, square, 1)
    isub = lax.broadcasted_iota(jnp.int32, square, 0)

    def holder(slots):
        found = jnp.where(slots >= 0, 0, -1)
        for u in range(1, n_scen):
            found = found + jnp.where(slots >= u * tiles, 1, 0)
        return found

    own_a, own_d = holder(across), holder(down)
    same = own_a == own_d
    rank_col = jnp.sum(jnp.where(same & (ilane < isub), 1, 0), axis=1, keepdims=True)
    rank_row = jnp.sum(jnp.where(same & (isub < ilane), 1, 0), axis=0, keepdims=True)
    key_col = jnp.where(isub < tiles, own_d * per + rank_col, -1)
    wanted = jnp.sum(
        jnp.where(key_col == ilane, down - own_d * tiles, 0), axis=0, keepdims=True
    )
    myreq[...] = jnp.broadcast_to(wanted, myreq.shape)
    keys_ref[...] = jnp.broadcast_to(own_a[0:1, :] * per + rank_row, keys_ref.shape)

    pl.semaphore_wait(barrier, n_dom - 1 + n_scen - 1)
    scen_peers(lambda u: req_copy(u, s).start())

    for name in ("count", "rows", "hot", "emb"):
        loads[name].wait()

    def row_of(index, columns):
        block_of = rows_ref[:, columns]
        at = lax.broadcasted_iota(jnp.int32, block_of.shape, 0)
        return jnp.sum(jnp.where(at == index, block_of, 0), axis=0, keepdims=True)

    def halo_group(group):
        first = group * per_group
        columns = []
        for half in range(GROUP // LANES):
            if cap >= LANES:
                parts = cap // LANES
                assert per_group == 1 and parts == GROUP // LANES
                row = row_of(first, slice(half * LANES, (half + 1) * LANES))
                limit = count_ref[first]
                place = lax.broadcasted_iota(jnp.int32, (1, LANES), 1) + half * LANES
                row = jnp.where(place < limit, row, -1)
            else:
                parts = LANES // cap
                row = row_of(group * (GROUP // LANES) + half, slice(0, LANES))
                place = lax.broadcasted_iota(jnp.int32, (1, LANES), 1)
                live = place < 0
                for i in range(parts):
                    limit = count_ref[first + half * parts + i]
                    live = live | ((place >= i * cap) & (place < i * cap + limit) & (place < (i + 1) * cap))
                row = jnp.where(live, row, -1)
            columns.append(spread(row)[1])
        out_buf[pl.ds(group * (GROUP // LANES), GROUP // LANES)] = picked_rows(
            jnp.concatenate(columns, axis=0), emb_ref
        ).reshape(GROUP // LANES, LANES, width)

    def halo_start(group):
        halo_group(group)
        if per_group == 1:
            halo_copy(group, d).start()
            return

        def step(i, carry):
            p = group * per_group + i

            @pl.when(p != d)
            def _():
                halo_copy(p, d).start()

            return carry

        lax.fori_loop(0, per_group, step, 0)

    my_group = d // per_group
    half_way = n_groups // 2
    order = []
    for k in range(half_way - 1, 0, -1):
        far, near = flipped(my_group, k + half_way), flipped(my_group, k)
        order.append(far + (near - far) * (s % 2))
        order.append(near + (far - near) * (s % 2))
    order.append(flipped(my_group, half_way))
    halo_start(order[0])

    r_ids, c_ids = spread(hot_ref[...])
    r_own, c_own = whole_part(r_ids, rows), whole_part(c_ids, rows)
    equal = r_ids == c_ids
    new_col = 1.0 - jnp.max(jnp.where(equal & (lane < sub), 1.0, 0.0), axis=1, keepdims=True)
    new_row = 1.0 - jnp.max(jnp.where(equal & (sub < lane), 1.0, 0.0), axis=0, keepdims=True)
    alike = r_own == c_own
    hot_rank_row = jnp.sum(
        jnp.where(alike & (c_ids < r_ids), new_col, 0.0), axis=0, keepdims=True
    )
    hot_rank_col = jnp.sum(
        jnp.where(alike & (r_ids < c_ids), new_row, 0.0), axis=1, keepdims=True
    )
    me = (d * n_scen + s).astype(jnp.float32)
    own_rows = picked_rows(c_ids - me * float(rows), emb_ref)
    chosen = jnp.where(
        (iota_f32((PAD, LANES), 0) == hot_rank_row) & (r_own[0:1, :] == me), new_row, 0.0
    ).astype(jnp.bfloat16)
    mine[...] = jnp.dot(chosen, own_rows, preferred_element_type=jnp.float32).astype(jnp.bfloat16)
    block(gat1, d, PAD)[...] = mine[...]
    dom_peers(lambda p: d1_copy(p, d).start())

    halo_start(order[1])

    scen_peers(lambda u: req_copy(u, u).wait_recv())
    reqs[pl.ds(s, 1)] = myreq[...][None]
    fetch = pltpu.make_async_copy(reqs, reqs_smem, own_sem.at[0])
    fetch.start()
    fetch.wait()

    def stage_for(u):
        for r in range(per):
            slot = reqs_smem[u, 0, s * per + r]
            stage[pl.ds(u * per + r, 1)] = emb_ref[slot][None]

    def serve(u):
        stage_for(u)
        loc_copy(u, s).start()

    scen_peers(serve)
    scen_peers(lambda u: w1_copy(u, s).start())
    scen_peers(lambda u: w2_copy(u, s).start())
    stage_for(s)
    local_ref[pl.ds(s * per, per)] = stage[pl.ds(s * per, per)]

    for group in order[2:]:
        halo_start(group)
    if per_group == 1:
        halo_group(my_group)
    else:
        halo_start(my_group)
    halo_place(d)[...] = halo_source(d)[...]

    dom_peers(lambda p: d1_copy(p, p).wait_recv())
    scen_peers(lambda u: d2_copy(u, s).start())
    block(gat2, s, drv_rows)[...] = gat1[...]
    scen_peers(lambda u: d2_copy(u, u).wait_recv())
    c_dom = whole_part(c_own, n_scen)
    place = (c_own - c_dom * float(n_scen)) * float(drv_rows) + c_dom * float(PAD) + hot_rank_col
    total = jnp.zeros(drv_ref.shape, jnp.float32)
    for at in range(0, n_scen * drv_rows, LANES):
        pick = jnp.where(place == lane + float(at), 1.0, 0.0).astype(jnp.bfloat16)
        total += jnp.dot(pick, gat2[at : at + LANES, :], preferred_element_type=jnp.float32)
    drv_ref[...] = total.astype(jnp.bfloat16)


    for name in ("feats", "fw", "b1", "w1", "w2", "b2", "dw", "adj", "halo_slot"):
        loads[name].wait()
    scen_peers(lambda u: w1_copy(u, u).wait())
    scen_peers(lambda u: w2_copy(u, u).wait())
    count = 4 if tiles % 4 == 0 else 1
    part = count * tile

    def own_part(i, carry):
        here = pl.ds(pl.multiple_of(i * part, part), part)
        inner = jnp.dot(
            emb_ref[pl.ds(i * count, count)].reshape(part, width),
            w1f_ref[:width, :],
            preferred_element_type=jnp.float32,
        )
        inner += lax.dot_general(
            feats_ref[:, here],
            fw_ref[...],
            (((0,), (0,)), ((), ())),
            preferred_element_type=jnp.float32,
        )
        inner_ref[here, :] = inner + b1_ref[...]
        return carry

    lax.fori_loop(0, tiles // count, own_part, 0)

    scen_peers(lambda u: loc_copy(u, u).wait())
    keys_copy = pltpu.make_async_copy(keys_ref, keys_smem, own_sem.at[1])
    keys_copy.start()
    keys_copy.wait()

    def local_part(i, carry):
        weights = jnp.concatenate([adj_ref[i, 0], dw_ref[i]], axis=1)
        sources = jnp.concatenate([local_ref[keys_smem[0, i]], drv_ref[...]], axis=0)
        agg_ref[i] = jnp.dot(weights, sources, preferred_element_type=jnp.float32)
        return carry

    lax.fori_loop(0, tiles, local_part, 0)

    dom_peers(lambda p: d1_copy(p, p).wait_send())
    for make in (req_copy, d2_copy):
        scen_peers(lambda u: make(u, u).wait_send())
    dom_peers(lambda p: halo_copy(p, p).wait())

    def result_copy(i):
        here = pl.ds(pl.multiple_of(i * part, part), part)
        return pltpu.make_async_copy(
            result_ref.at[here], result_hbm.at[here], result_sem.at[i]
        )

    def last_part(i, carry):
        here = pl.ds(pl.multiple_of(i * part, part), part)
        totals = []
        for j in range(count):
            t = i * count + j
            total = agg_ref[t] + jnp.dot(
                adj_ref[t, 1], halo_ref[halo_slot_ref[t]], preferred_element_type=jnp.float32
            )
            totals.append(total.astype(jnp.bfloat16))
        inner = inner_ref[here, :] + jnp.dot(
            jnp.concatenate(totals, axis=0),
            w1f_ref[width:, :],
            preferred_element_type=jnp.float32,
        )
        activated = (0.5 * inner * (1.0 + lax.erf(inner * (0.5**0.5)))).astype(jnp.bfloat16)
        result = jnp.dot(activated, w2f_ref[...], preferred_element_type=jnp.float32)
        own = emb_ref[pl.ds(i * count, count)].reshape(part, width).astype(jnp.float32)
        result_ref[here, :] = (result + (own + b2_ref[...])).astype(jnp.bfloat16)
        result_copy(i).start()
        return carry

    lax.fori_loop(0, tiles // count, last_part, 0)

    def finish(i, carry):
        result_copy(i).wait()
        return carry

    lax.fori_loop(0, tiles // count, finish, 0)


def per_device(
    embedding,
    scenario_feats,
    adjacency,
    driver_weight,
    local_slot,
    halo_slot,
    send_rows,
    send_count,
    hot_ids,
    first_weight,
    feature_weight,
    first_bias,
    second_weight,
    second_bias,
):
    n_dom, n_scen = lax.axis_size("dom"), lax.axis_size("scen")
    rows, width = embedding.shape
    tiles, _, tile, _ = adjacency.shape
    slots, cap = send_rows.size, send_rows.shape[1]
    hot = hot_ids.shape[0]
    assert -(-hot // (n_dom * n_scen)) <= PAD and tile == LANES
    if cap < LANES:
        send_rows = send_rows.reshape(-1, LANES)
    bf16, f32, i32 = jnp.bfloat16, jnp.float32, jnp.int32
    vmem, smem, dma = pltpu.VMEM, pltpu.SMEM, pltpu.SemaphoreType.DMA
    anywhere = pl.BlockSpec(memory_space=pl.ANY)
    operands = (
        hot_ids.reshape(1, -1),
        local_slot.reshape(1, -1),
        halo_slot,
        send_rows,
        send_count,
        embedding.reshape(tiles, tile, width),
        scenario_feats,
        adjacency,
        driver_weight.reshape(tiles, tile, hot),
        first_weight,
        feature_weight,
        first_bias.reshape(1, -1),
        second_weight,
        second_bias.reshape(1, -1),
    )
    by_dom = [dma((n_dom,)), dma((n_dom,))]
    by_scen = [dma((n_scen,)), dma((n_scen,))]
    return pl.pallas_call(
        functools.partial(layer_kernel, n_dom, n_scen, cap),
        out_shape=jax.ShapeDtypeStruct((rows, width), bf16),
        in_specs=[anywhere] * len(operands),
        out_specs=anywhere,
        scratch_shapes=[
            vmem((1, hot), i32),
            vmem((1, tiles), i32),
            smem(halo_slot.shape, i32),
            vmem(send_rows.shape, i32),
            smem(send_count.shape, i32),
            vmem((tiles, tile, width), bf16),
            vmem(scenario_feats.shape, bf16),
            vmem(adjacency.shape, bf16),
            vmem((tiles, tile, hot), bf16),
            vmem(feature_weight.shape, bf16),
            vmem((1, width), f32),
            vmem((1, width), f32),
            vmem((n_scen * first_weight.shape[0], width), bf16),
            vmem((n_scen * second_weight.shape[0], width), bf16),
            vmem((slots // tile, tile, width), bf16),
            vmem((tiles, tile, width), bf16),
            vmem((hot, width), bf16),
            vmem((8, LANES), i32),
            smem((8, LANES), i32),
            vmem((slots // tile, tile, width), bf16),
            vmem((tiles, tile, width), bf16),
            vmem((8, LANES), i32),
            vmem((n_scen, 8, LANES), i32),
            smem((n_scen, 8, LANES), i32),
            vmem((PAD, width), bf16),
            vmem((n_dom * PAD, width), bf16),
            vmem((n_scen * n_dom * PAD, width), bf16),
            vmem((8, LANES), i32),
            vmem((tiles, tile, width), f32),
            vmem((rows, width), f32),
            vmem((rows, width), bf16),
            dma((len(operands),)),
            *by_dom,
            *by_scen,
            *by_scen,
            *by_dom,
            *by_scen,
            *by_scen,
            *by_scen,
            dma((2,)),
            dma((tiles,)),
        ],
        compiler_params=pltpu.CompilerParams(
            collective_id=0, has_side_effects=True, vmem_limit_bytes=60 * 1024 * 1024
        ),
        name="layer",
    )(*operands)


def solution(mesh):
    return jax.shard_map(
        per_device,
        mesh=mesh,
        in_specs=(
            P(("dom", "scen"), None),
            P(None, ("dom", "scen")),
            P(("dom", "scen"), None, None, None),
            P(("dom", "scen"), None),
            P(("dom", "scen")),
            P(("dom", "scen")),
            P(("dom", "scen"), None),
            P(("dom", "scen")),
            P(),
            P("scen", None),
            P(),
            P(),
            P("scen", None),
            P(),
        ),
        out_specs=P(("dom", "scen"), None),
        check_vma=False,
    )
```

time: 47.7 us -> 45.5 us (0.954)
  local copies, waits for them, and re-layouts: 8.02 us -> 2.46 us
  Pallas kernels: 39.2 us -> 42.9 us
    unnamed x30 -> x1, local copies, waits for them, and re-layouts: 8.02 us -> 2.46 us
    pallas_call x2 -> x1, Pallas kernels: 39.2 us -> 42.9 us  [per_device(): pl.pallas_call(functools.partial(layer_kernel, n_dom, n_scen, cap), out_s...]
where the time goes in v2:
time: 45.5 us; the launch traced here: 45.3 us
  Pallas kernels  42.9 us (94%)
  local copies, waits for them, and re-layouts  2.46 us (5%)
    pallas_call x1, Pallas kernels, per_device(): pl.pallas_call(functools.partial(layer_kernel, n_dom, n_scen, cap), out_s...  42.9 us
    unnamed x1, local copies, waits for them, and re-layouts  2.46 us

profile of v2, /device:TPU:0, one launch (start us, length us, event | category | flops | bytes accessed | tf_op | source)
XLA Modules:
  0.0 45.3 jit_solution(7224583214663327218)
XLA Ops:
  0.0 42.9 %layer.1 = bf16[2560,256]{1,0:T(8,128)(2,1)} custom-call(s32[1,128]{1,0:T(1,128)} %bitcast.10, s32[1,20]{1,0:T(1,128)} %bitcast.11, s32[20]{0:T(128)} %halo_slot_hbm.1, s32[8,256]{1,0:T(8,128)} %rows_hbm.1, s32[8]{0:T(128)} %count_hbm.1, bf16[20,128,256]{2,1,0:T(8,128)(2,1)} %bitcast.6, bf16[16,2560]{1,0:T(8,128)(2,1)} %feats_hbm.1, ...), custom_call_target="tpu_custom_call" | custom-call | tf_op jit(solution)/shard_map/layer/pallas_call | solution.py:534
  42.9 2.5 %copy.16 = bf16[2560,256]{1,0:T(8,128)(2,1)} copy(bf16[2560,256]{1,0:T(8,128)(2,1)} %layer.1) | data formatting | bytes 2621440

commit v3 on v2

--- a/solution.py
+++ b/solution.py
@@ -50,13 +50,13 @@
     ).astype(jnp.bfloat16)
 
 
-def layer_kernel(
+def gather_kernel(
     n_dom,
     n_scen,
     cap,
+    hot_cap,
     hot_hbm,
     slot_hbm,
-    halo_slot_hbm,
     rows_hbm,
     count_hbm,
     emb_hbm,
@@ -67,11 +67,12 @@
     fw_hbm,
     b1_hbm,
     w2_hbm,
-    b2_hbm,
-    result_hbm,
+    halo_ref,
+    inner_hbm,
+    w1b_hbm,
+    w2f_hbm,
     hot_ref,
     slot_ref,
-    halo_slot_ref,
     rows_ref,
     count_ref,
     emb_ref,
@@ -80,10 +81,8 @@
     dw_ref,
     fw_ref,
     b1_ref,
-    b2_ref,
     w1f_ref,
     w2f_ref,
-    halo_ref,
     local_ref,
     drv_ref,
     keys_ref,
@@ -97,9 +96,7 @@
     gat1,
     gat2,
     padrow,
-    agg_ref,
     inner_ref,
-    result_ref,
     in_sem,
     halo_send,
     halo_recv,
@@ -116,7 +113,7 @@
     w2_send,
     w2_recv,
     own_sem,
-    result_sem,
+    inner_sem,
 ):
     d = lax.axis_index("dom")
     s = lax.axis_index("scen")
@@ -125,7 +122,7 @@
     per = tiles // n_scen
     per_group = max(1, GROUP // cap)
     n_groups = n_dom // per_group
-    drv_rows = n_dom * PAD
+    drv_rows = n_dom * hot_cap
 
     def dom_peers(body):
         def step(k, carry):
@@ -193,28 +190,40 @@
             mine, block(gat1, mark, PAD), d1_send.at[peer], d1_recv.at[mark], {"dom": peer}
         )
 
-    def d2_copy(peer, mark):
-        return remote(
-            gat1, block(gat2, mark, drv_rows), d2_send.at[peer], d2_recv.at[mark], {"scen": peer}
-        )
-
-    def w1_copy(peer, mark):
-        return remote(
-            w1_hbm,
-            block(w1f_ref, mark, w1_hbm.shape[0]),
-            w1_send.at[peer],
-            w1_recv.at[mark],
-            {"scen": peer},
-        )
-
-    def w2_copy(peer, mark):
-        return remote(
-            w2_hbm,
-            block(w2f_ref, mark, w2_hbm.shape[0]),
-            w2_send.at[peer],
-            w2_recv.at[mark],
-            {"scen": peer},
-        )
+    doubling = []
+    held, mask = [0], n_scen // 2
+    while mask:
+        doubling.append([(mask, k) for k in held])
+        held, mask = held + [k + mask for k in held], mask // 2
+
+    def doubled(ref, send, recv, mask, k):
+        part = block(ref, flipped(s, k), ref.shape[0] // n_scen)
+        at = (n_scen // (2 * mask) - 1) + held.index(k)
+        return remote(part, part, send.at[at], recv.at[at], {"scen": flipped(s, mask)})
+
+    def arriving(ref, send, recv, mask, k):
+        part = block(ref, flipped(s, k + mask), ref.shape[0] // n_scen)
+        at = (n_scen // (2 * mask) - 1) + held.index(k)
+        return remote(part, part, send.at[at], recv.at[at], {"scen": flipped(s, mask)})
+
+    both_weights = ((w1f_ref, w1_send, w1_recv), (w2f_ref, w2_send, w2_recv))
+    drivers = ((gat2, d2_send, d2_recv),)
+
+    def start_step(arrays, step):
+        for mask, k in doubling[step]:
+            for array in arrays:
+                doubled(*array, mask, k).start()
+
+    def wait_step(arrays, step):
+        for mask, k in doubling[step]:
+            for array in arrays:
+                arriving(*array, mask, k).wait_recv()
+
+    def sent(arrays):
+        for steps in doubling:
+            for mask, k in steps:
+                for array in arrays:
+                    doubled(*array, mask, k).wait_send()
 
     loads = {}
 
@@ -223,10 +232,15 @@
         loads[name].start()
 
     load("slot", slot_hbm, slot_ref)
+    load("w1", w1_hbm, block(w1f_ref, s, w1_hbm.shape[0]))
+    load("w2", w2_hbm, block(w2f_ref, s, w2_hbm.shape[0]))
     load("count", count_hbm, count_ref)
     load("rows", rows_hbm, rows_ref)
     load("hot", hot_hbm, hot_ref)
-    load("emb", emb_hbm, emb_ref)
+    quarter = tiles // 4
+    for i in range(4):
+        piece = pl.ds(i * quarter, quarter)
+        load(f"emb{i}", emb_hbm.at[piece], emb_ref.at[piece])
 
     barrier = pltpu.get_barrier_semaphore()
     dom_peers(
@@ -240,13 +254,9 @@
         )
     )
 
-    load("halo_slot", halo_slot_hbm, halo_slot_ref)
-    load("w1", w1_hbm, block(w1f_ref, s, w1_hbm.shape[0]))
-    load("w2", w2_hbm, block(w2f_ref, s, w2_hbm.shape[0]))
     load("feats", feats_hbm, feats_ref)
     load("fw", fw_hbm, fw_ref)
     load("b1", b1_hbm, b1_ref)
-    load("b2", b2_hbm, b2_ref)
     load("dw", dw_hbm, dw_ref)
     load("adj", adj_hbm, adj_ref)
 
@@ -281,8 +291,11 @@
 
     pl.semaphore_wait(barrier, n_dom - 1 + n_scen - 1)
     scen_peers(lambda u: req_copy(u, s).start())
-
-    for name in ("count", "rows", "hot", "emb"):
+    loads["w1"].wait()
+    loads["w2"].wait()
+    start_step(both_weights, 0)
+
+    for name in ("count", "rows", "hot", "emb0", "emb1", "emb2", "emb3"):
         loads[name].wait()
 
     def row_of(index, columns):
@@ -342,6 +355,27 @@
     order.append(flipped(my_group, half_way))
     halo_start(order[0])
 
+    scen_peers(lambda u: req_copy(u, u).wait_recv())
+    reqs[pl.ds(s, 1)] = myreq[...][None]
+    fetch = pltpu.make_async_copy(reqs, reqs_smem, own_sem.at[0])
+    fetch.start()
+    fetch.wait()
+
+    def stage_for(u):
+        for r in range(per):
+            slot = reqs_smem[u, 0, s * per + r]
+            stage[pl.ds(u * per + r, 1)] = emb_ref[slot][None]
+
+    def serve(u):
+        stage_for(u)
+        loc_copy(u, s).start()
+
+    scen_peers(serve)
+    stage_for(s)
+    local_ref[pl.ds(s * per, per)] = stage[pl.ds(s * per, per)]
+
+    halo_start(order[1])
+
     r_ids, c_ids = spread(hot_ref[...])
     r_own, c_own = whole_part(r_ids, rows), whole_part(c_ids, rows)
     equal = r_ids == c_ids
@@ -363,43 +397,35 @@
     block(gat1, d, PAD)[...] = mine[...]
     dom_peers(lambda p: d1_copy(p, d).start())
 
-    halo_start(order[1])
-
-    scen_peers(lambda u: req_copy(u, u).wait_recv())
-    reqs[pl.ds(s, 1)] = myreq[...][None]
-    fetch = pltpu.make_async_copy(reqs, reqs_smem, own_sem.at[0])
-    fetch.start()
-    fetch.wait()
-
-    def stage_for(u):
-        for r in range(per):
-            slot = reqs_smem[u, 0, s * per + r]
-            stage[pl.ds(u * per + r, 1)] = emb_ref[slot][None]
-
-    def serve(u):
-        stage_for(u)
-        loc_copy(u, s).start()
-
-    scen_peers(serve)
-    scen_peers(lambda u: w1_copy(u, s).start())
-    scen_peers(lambda u: w2_copy(u, s).start())
-    stage_for(s)
-    local_ref[pl.ds(s * per, per)] = stage[pl.ds(s * per, per)]
-
     for group in order[2:]:
         halo_start(group)
     if per_group == 1:
         halo_group(my_group)
     else:
         halo_start(my_group)
-    halo_place(d)[...] = halo_source(d)[...]
+    own_halo = pltpu.make_async_copy(halo_source(d), halo_place(d), own_sem.at[2])
+    own_halo.start()
+
+    wait_step(both_weights, 0)
+    start_step(both_weights, 1)
 
     dom_peers(lambda p: d1_copy(p, p).wait_recv())
-    scen_peers(lambda u: d2_copy(u, s).start())
-    block(gat2, s, drv_rows)[...] = gat1[...]
-    scen_peers(lambda u: d2_copy(u, u).wait_recv())
+    at_row = iota_f32((drv_rows, n_dom * PAD), 0)
+    at_dom = whole_part(at_row, hot_cap)
+    keep = at_dom * float(PAD) + (at_row - at_dom * float(hot_cap))
+    keep = jnp.where(keep == iota_f32(keep.shape, 1), 1.0, 0.0).astype(jnp.bfloat16)
+    block(gat2, s, drv_rows)[...] = jnp.dot(
+        keep, gat1[...], preferred_element_type=jnp.float32
+    ).astype(jnp.bfloat16)
+    for step in range(len(doubling)):
+        start_step(drivers, step)
+        wait_step(drivers, step)
+    for step in range(1, len(doubling)):
+        wait_step(both_weights, step)
+        if step + 1 < len(doubling):
+            start_step(both_weights, step + 1)
     c_dom = whole_part(c_own, n_scen)
-    place = (c_own - c_dom * float(n_scen)) * float(drv_rows) + c_dom * float(PAD) + hot_rank_col
+    place = (c_own - c_dom * float(n_scen)) * float(drv_rows) + c_dom * float(hot_cap) + hot_rank_col
     total = jnp.zeros(drv_ref.shape, jnp.float32)
     for at in range(0, n_scen * drv_rows, LANES):
         pick = jnp.where(place == lane + float(at), 1.0, 0.0).astype(jnp.bfloat16)
@@ -407,12 +433,24 @@
     drv_ref[...] = total.astype(jnp.bfloat16)
 
 
-    for name in ("feats", "fw", "b1", "w1", "w2", "b2", "dw", "adj", "halo_slot"):
+    for name in ("feats", "fw", "b1", "dw", "adj"):
         loads[name].wait()
-    scen_peers(lambda u: w1_copy(u, u).wait())
-    scen_peers(lambda u: w2_copy(u, u).wait())
+    scen_peers(lambda u: loc_copy(u, u).wait())
+    to_out = [
+        pltpu.make_async_copy(w1f_ref.at[pl.ds(width, width)], w1b_hbm, own_sem.at[3]),
+        pltpu.make_async_copy(w2f_ref, w2f_hbm, own_sem.at[4]),
+    ]
+    for copy in to_out:
+        copy.start()
+    keys_copy = pltpu.make_async_copy(keys_ref, keys_smem, own_sem.at[1])
+    keys_copy.start()
+    keys_copy.wait()
     count = 4 if tiles % 4 == 0 else 1
     part = count * tile
+
+    def inner_copy(i):
+        here = pl.ds(pl.multiple_of(i * part, part), part)
+        return pltpu.make_async_copy(inner_ref.at[here], inner_hbm.at[here], inner_sem.at[i])
 
     def own_part(i, carry):
         here = pl.ds(pl.multiple_of(i * part, part), part)
@@ -427,63 +465,88 @@
             (((0,), (0,)), ((), ())),
             preferred_element_type=jnp.float32,
         )
-        inner_ref[here, :] = inner + b1_ref[...]
-        return carry
-
-    lax.fori_loop(0, tiles // count, own_part, 0)
-
-    scen_peers(lambda u: loc_copy(u, u).wait())
-    keys_copy = pltpu.make_async_copy(keys_ref, keys_smem, own_sem.at[1])
-    keys_copy.start()
-    keys_copy.wait()
-
-    def local_part(i, carry):
-        weights = jnp.concatenate([adj_ref[i, 0], dw_ref[i]], axis=1)
-        sources = jnp.concatenate([local_ref[keys_smem[0, i]], drv_ref[...]], axis=0)
-        agg_ref[i] = jnp.dot(weights, sources, preferred_element_type=jnp.float32)
-        return carry
-
-    lax.fori_loop(0, tiles, local_part, 0)
-
-    dom_peers(lambda p: d1_copy(p, p).wait_send())
-    for make in (req_copy, d2_copy):
-        scen_peers(lambda u: make(u, u).wait_send())
-    dom_peers(lambda p: halo_copy(p, p).wait())
-
-    def result_copy(i):
-        here = pl.ds(pl.multiple_of(i * part, part), part)
-        return pltpu.make_async_copy(
-            result_ref.at[here], result_hbm.at[here], result_sem.at[i]
-        )
-
-    def last_part(i, carry):
-        here = pl.ds(pl.multiple_of(i * part, part), part)
         totals = []
         for j in range(count):
             t = i * count + j
-            total = agg_ref[t] + jnp.dot(
-                adj_ref[t, 1], halo_ref[halo_slot_ref[t]], preferred_element_type=jnp.float32
-            )
+            weights = jnp.concatenate([adj_ref[t, 0], dw_ref[t]], axis=1)
+            sources = jnp.concatenate([local_ref[keys_smem[0, t]], drv_ref[...]], axis=0)
+            total = jnp.dot(weights, sources, preferred_element_type=jnp.float32)
             totals.append(total.astype(jnp.bfloat16))
-        inner = inner_ref[here, :] + jnp.dot(
+        inner += jnp.dot(
             jnp.concatenate(totals, axis=0),
             w1f_ref[width:, :],
             preferred_element_type=jnp.float32,
         )
-        activated = (0.5 * inner * (1.0 + lax.erf(inner * (0.5**0.5)))).astype(jnp.bfloat16)
-        result = jnp.dot(activated, w2f_ref[...], preferred_element_type=jnp.float32)
-        own = emb_ref[pl.ds(i * count, count)].reshape(part, width).astype(jnp.float32)
-        result_ref[here, :] = (result + (own + b2_ref[...])).astype(jnp.bfloat16)
-        result_copy(i).start()
+        inner_ref[here, :] = inner + b1_ref[...]
+        inner_copy(i).start()
         return carry
 
-    lax.fori_loop(0, tiles // count, last_part, 0)
+    lax.fori_loop(0, tiles // count, own_part, 0)
+
+    dom_peers(lambda p: d1_copy(p, p).wait_send())
+    scen_peers(lambda u: req_copy(u, u).wait_send())
+    sent(both_weights)
+    sent(drivers)
+    own_halo.wait()
+    for copy in to_out:
+        copy.wait()
 
     def finish(i, carry):
-        result_copy(i).wait()
+        inner_copy(i).wait()
         return carry
 
     lax.fori_loop(0, tiles // count, finish, 0)
+    dom_peers(lambda p: halo_copy(p, p).wait())
+
+
+def update_kernel(
+    count, slot_ref, emb_ref, adj_ref, inner_ref, halo_ref, w1b_ref, w2_ref, b2_ref, out_ref
+):
+    step = pl.program_id(0)
+    totals = []
+    for j in range(count):
+        halo = halo_ref[slot_ref[step * count + j]]
+        total = jnp.dot(adj_ref[j, 0], halo, preferred_element_type=jnp.float32)
+        totals.append(total.astype(jnp.bfloat16))
+    inner = inner_ref[...] + jnp.dot(
+        jnp.concatenate(totals, axis=0), w1b_ref[...], preferred_element_type=jnp.float32
+    )
+    activated = (0.5 * inner * (1.0 + lax.erf(inner * (0.5**0.5)))).astype(jnp.bfloat16)
+    result = jnp.dot(activated, w2_ref[...], preferred_element_type=jnp.float32)
+    out_ref[...] = (result + (emb_ref[...].astype(jnp.float32) + b2_ref[...])).astype(
+        jnp.bfloat16
+    )
+
+
+def update(halo_slot, embedding, adjacency, inner, halo, w1b, w2, b2):
+    rows, width = embedding.shape
+    tiles, _, tile, _ = adjacency.shape
+    count = 4 if tiles % 4 == 0 else 1
+    part = count * tile
+
+    def all_of(array):
+        return pl.BlockSpec(array.shape, lambda i, *_: (0,) * array.ndim)
+
+    return pl.pallas_call(
+        functools.partial(update_kernel, count),
+        grid_spec=pltpu.PrefetchScalarGridSpec(
+            num_scalar_prefetch=1,
+            grid=(tiles // count,),
+            in_specs=[
+                pl.BlockSpec((part, width), lambda i, *_: (i, 0)),
+                pl.BlockSpec((count, 1, tile, tile), lambda i, *_: (i, 1, 0, 0)),
+                pl.BlockSpec((part, width), lambda i, *_: (i, 0)),
+                all_of(halo),
+                all_of(w1b),
+                all_of(w2),
+                all_of(b2),
+            ],
+            out_specs=pl.BlockSpec((part, width), lambda i, *_: (i, 0)),
+        ),
+        out_shape=jax.ShapeDtypeStruct((rows, width), jnp.bfloat16),
+        compiler_params=pltpu.CompilerParams(vmem_limit_bytes=60 * 1024 * 1024),
+        name="update",
+    )(halo_slot, embedding, adjacency, inner, halo, w1b, w2, b2)
 
 
 def per_device(
@@ -507,7 +570,8 @@
     tiles, _, tile, _ = adjacency.shape
     slots, cap = send_rows.size, send_rows.shape[1]
     hot = hot_ids.shape[0]
-    assert -(-hot // (n_dom * n_scen)) <= PAD and tile == LANES
+    hot_cap = -(-hot // (n_dom * n_scen))
+    assert hot_cap <= PAD and tile == LANES
     if cap < LANES:
         send_rows = send_rows.reshape(-1, LANES)
     bf16, f32, i32 = jnp.bfloat16, jnp.float32, jnp.int32
@@ -516,7 +580,6 @@
     operands = (
         hot_ids.reshape(1, -1),
         local_slot.reshape(1, -1),
-        halo_slot,
         send_rows,
         send_count,
         embedding.reshape(tiles, tile, width),
@@ -527,19 +590,22 @@
         feature_weight,
         first_bias.reshape(1, -1),
         second_weight,
-        second_bias.reshape(1, -1),
     )
     by_dom = [dma((n_dom,)), dma((n_dom,))]
     by_scen = [dma((n_scen,)), dma((n_scen,))]
-    return pl.pallas_call(
-        functools.partial(layer_kernel, n_dom, n_scen, cap),
-        out_shape=jax.ShapeDtypeStruct((rows, width), bf16),
+    halo, inner, w1b, w2 = pl.pallas_call(
+        functools.partial(gather_kernel, n_dom, n_scen, cap, hot_cap),
+        out_shape=(
+            jax.ShapeDtypeStruct((slots // tile, tile, width), bf16),
+            jax.ShapeDtypeStruct((rows, width), f32),
+            jax.ShapeDtypeStruct((width, width), bf16),
+            jax.ShapeDtypeStruct((width, width), bf16),
+        ),
         in_specs=[anywhere] * len(operands),
-        out_specs=anywhere,
+        out_specs=(anywhere,) * 4,
         scratch_shapes=[
             vmem((1, hot), i32),
             vmem((1, tiles), i32),
-            smem(halo_slot.shape, i32),
             vmem(send_rows.shape, i32),
             smem(send_count.shape, i32),
             vmem((tiles, tile, width), bf16),
@@ -548,10 +614,8 @@
             vmem((tiles, tile, hot), bf16),
             vmem(feature_weight.shape, bf16),
             vmem((1, width), f32),
-            vmem((1, width), f32),
             vmem((n_scen * first_weight.shape[0], width), bf16),
             vmem((n_scen * second_weight.shape[0], width), bf16),
-            vmem((slots // tile, tile, width), bf16),
             vmem((tiles, tile, width), bf16),
             vmem((hot, width), bf16),
             vmem((8, LANES), i32),
@@ -563,12 +627,10 @@
             smem((n_scen, 8, LANES), i32),
             vmem((PAD, width), bf16),
             vmem((n_dom * PAD, width), bf16),
-            vmem((n_scen * n_dom * PAD, width), bf16),
+            vmem((n_scen * n_dom * hot_cap, width), bf16),
             vmem((8, LANES), i32),
-            vmem((tiles, tile, width), f32),
             vmem((rows, width), f32),
-            vmem((rows, width), bf16),
-            dma((len(operands),)),
+            dma((len(operands) + 3,)),
             *by_dom,
             *by_scen,
             *by_scen,
@@ -576,14 +638,17 @@
             *by_scen,
             *by_scen,
             *by_scen,
-            dma((2,)),
+            dma((5,)),
             dma((tiles,)),
         ],
         compiler_params=pltpu.CompilerParams(
             collective_id=0, has_side_effects=True, vmem_limit_bytes=60 * 1024 * 1024
         ),
-        name="layer",
+        name="gather",
     )(*operands)
+    return update(
+        halo_slot, embedding, adjacency, inner, halo, w1b, w2, second_bias.reshape(1, -1)
+    )
 
 
 def solution(mesh):

time: 45.5 us -> 41.1 us (0.903); the launches traced: 45.3 us -> 40.4 us
  Pallas kernels: 42.9 us -> 40.4 us
  local copies, waits for them, and re-layouts: 2.46 us -> 0 us
    unnamed x1 -> x0, local copies, waits for them, and re-layouts: 2.46 us -> none
    pallas_call x1 -> x2, Pallas kernels: 42.9 us -> 40.4 us  [the longest x1 33.3 us: per_device(): pl.pallas_call(functools.partial(gather_kernel, n_dom, n_scen, cap, hot_c...]
where the time goes in v3:
time: 41.1 us; the launch traced here: 40.4 us
  Pallas kernels  40.4 us (98%)
    pallas_call x1, Pallas kernels, per_device(): pl.pallas_call(functools.partial(gather_kernel, n_dom, n_scen, cap, hot_c...  33.3 us
    pallas_call x1, Pallas kernels, update(): pl.pallas_call(functools.partial(update_kernel, count), grid_spec=pltpu.P...  7.17 us

profile of v3, /device:TPU:0, one launch (start us, length us, event | category | flops | bytes accessed | tf_op | source)
XLA Modules:
  0.0 40.4 jit_solution(16037921522170048948)
XLA Ops:
  0.0 33.3 %gather.1 = (bf16[16,128,256]{2,1,0:T(8,128)(2,1)}, f32[2560,256]{1,0:T(8,128)}, bf16[256,256]{1,0:T(8,128)(2,1)}, bf16[256,256]{1,0:T(8,128)(2,1)}) custom-call(s32[1,128]{1,0:T(1,128)} %bitcast.10, s32[1,20]{1,0:T(1,128)} %bitcast.11, s32[8,256]{1,0:T(8,128)} %rows_hbm.1, s32[8]{0:T(128)} %count_hbm.1, bf16[20,128,256]{2,1,0:T(8,128)(2,1)} %bitcast.6, ...), custom_call_target="tpu_custom_call" | custom-call | tf_op jit(solution)/shard_map/gather/pallas_call | solution.py:596
  33.3 7.2 %update.1 = bf16[2560,256]{1,0:T(8,128)(2,1)} custom-call(s32[20]{0:T(128)} %slot_ref.1, bf16[2560,256]{1,0:T(8,128)(2,1)} %emb_ref.1, bf16[20,2,128,128]{3,2,1,0:T(8,128)(2,1)} %adj_ref.1, f32[2560,256]{1,0:T(8,128)} %get-tuple-element.9.inner_ref, bf16[16,128,256]{2,1,0:T(8,128)(2,1)} %get-tuple-element.10.halo_ref, ...), custom_call_target="tpu_custom_call" | custom-call | tf_op jit(solution)/shard_map/update/pallas_call | solution.py:530

commit v4 on v3

--- a/solution.py
+++ b/solution.py
@@ -420,10 +420,6 @@
     for step in range(len(doubling)):
         start_step(drivers, step)
         wait_step(drivers, step)
-    for step in range(1, len(doubling)):
-        wait_step(both_weights, step)
-        if step + 1 < len(doubling):
-            start_step(both_weights, step + 1)
     c_dom = whole_part(c_own, n_scen)
     place = (c_own - c_dom * float(n_scen)) * float(drv_rows) + c_dom * float(hot_cap) + hot_rank_col
     total = jnp.zeros(drv_ref.shape, jnp.float32)
@@ -433,8 +429,33 @@
     drv_ref[...] = total.astype(jnp.bfloat16)
 
 
+    for step in range(1, len(doubling)):
+        wait_step(both_weights, step)
+        if step + 1 < len(doubling):
+            start_step(both_weights, step + 1)
     for name in ("feats", "fw", "b1", "dw", "adj"):
         loads[name].wait()
+    count = 4 if tiles % 4 == 0 else 1
+    part = count * tile
+
+    def own_part(i, carry):
+        here = pl.ds(pl.multiple_of(i * part, part), part)
+        inner = jnp.dot(
+            emb_ref[pl.ds(i * count, count)].reshape(part, width),
+            w1f_ref[:width, :],
+            preferred_element_type=jnp.float32,
+        )
+        inner += lax.dot_general(
+            feats_ref[:, here],
+            fw_ref[...],
+            (((0,), (0,)), ((), ())),
+            preferred_element_type=jnp.float32,
+        )
+        inner_ref[here, :] = inner + b1_ref[...]
+        return carry
+
+    lax.fori_loop(0, tiles // count, own_part, 0)
+
     scen_peers(lambda u: loc_copy(u, u).wait())
     to_out = [
         pltpu.make_async_copy(w1f_ref.at[pl.ds(width, width)], w1b_hbm, own_sem.at[3]),
@@ -445,26 +466,13 @@
     keys_copy = pltpu.make_async_copy(keys_ref, keys_smem, own_sem.at[1])
     keys_copy.start()
     keys_copy.wait()
-    count = 4 if tiles % 4 == 0 else 1
-    part = count * tile
 
     def inner_copy(i):
         here = pl.ds(pl.multiple_of(i * part, part), part)
         return pltpu.make_async_copy(inner_ref.at[here], inner_hbm.at[here], inner_sem.at[i])
 
-    def own_part(i, carry):
+    def local_part(i, carry):
         here = pl.ds(pl.multiple_of(i * part, part), part)
-        inner = jnp.dot(
-            emb_ref[pl.ds(i * count, count)].reshape(part, width),
-            w1f_ref[:width, :],
-            preferred_element_type=jnp.float32,
-        )
-        inner += lax.dot_general(
-            feats_ref[:, here],
-            fw_ref[...],
-            (((0,), (0,)), ((), ())),
-            preferred_element_type=jnp.float32,
-        )
         totals = []
         for j in range(count):
             t = i * count + j
@@ -472,16 +480,15 @@
             sources = jnp.concatenate([local_ref[keys_smem[0, t]], drv_ref[...]], axis=0)
             total = jnp.dot(weights, sources, preferred_element_type=jnp.float32)
             totals.append(total.astype(jnp.bfloat16))
-        inner += jnp.dot(
+        inner_ref[here, :] += jnp.dot(
             jnp.concatenate(totals, axis=0),
             w1f_ref[width:, :],
             preferred_element_type=jnp.float32,
         )
-        inner_ref[here, :] = inner + b1_ref[...]
         inner_copy(i).start()
         return carry
 
-    lax.fori_loop(0, tiles // count, own_part, 0)
+    lax.fori_loop(0, tiles // count, local_part, 0)
 
     dom_peers(lambda p: d1_copy(p, p).wait_send())
     scen_peers(lambda u: req_copy(u, u).wait_send())
@@ -499,51 +506,116 @@
     dom_peers(lambda p: halo_copy(p, p).wait())
 
 
+def gelu(x):
+    size = jnp.abs(x)
+    t = 1.0 / (1.0 + (0.3275911 * 0.5**0.5) * size)
+    tail = 0.5 * 1.061405429
+    for factor in (-1.453152027, 1.421413741, -0.284496736, 0.254829592):
+        tail = tail * t + 0.5 * factor
+    tail = tail * t * jnp.exp2(x * x * (-0.5 * 1.4426950408889634))
+    return jnp.maximum(x, 0.0) - size * tail
+
+
 def update_kernel(
-    count, slot_ref, emb_ref, adj_ref, inner_ref, halo_ref, w1b_ref, w2_ref, b2_ref, out_ref
+    slot_ref,
+    emb_hbm,
+    adj_hbm,
+    inner_hbm,
+    halo_hbm,
+    w1b_hbm,
+    w2_hbm,
+    b2_ref,
+    out_hbm,
+    emb_ref,
+    adj_ref,
+    inner_ref,
+    halo_ref,
+    w1b_ref,
+    w2_ref,
+    result_ref,
+    part_sem,
+    halo_sem,
+    weight_sem,
+    out_sem,
 ):
-    step = pl.program_id(0)
-    totals = []
-    for j in range(count):
-        halo = halo_ref[slot_ref[step * count + j]]
-        total = jnp.dot(adj_ref[j, 0], halo, preferred_element_type=jnp.float32)
-        totals.append(total.astype(jnp.bfloat16))
-    inner = inner_ref[...] + jnp.dot(
-        jnp.concatenate(totals, axis=0), w1b_ref[...], preferred_element_type=jnp.float32
-    )
-    activated = (0.5 * inner * (1.0 + lax.erf(inner * (0.5**0.5)))).astype(jnp.bfloat16)
-    result = jnp.dot(activated, w2_ref[...], preferred_element_type=jnp.float32)
-    out_ref[...] = (result + (emb_ref[...].astype(jnp.float32) + b2_ref[...])).astype(
-        jnp.bfloat16
-    )
+    tiles, tile, _ = adj_ref.shape
+    count = 4 if tiles % 4 == 0 else 1
+    part = count * tile
+    steps = tiles // count
+
+    def started(src, dst, sem):
+        copy = pltpu.make_async_copy(src, dst, sem)
+        copy.start()
+        return copy
+
+    quarter = halo_ref.shape[0] // 4
+    ready = []
+    for i in range(4):
+        here = pl.ds(i * quarter, quarter)
+        ready.append(started(halo_hbm.at[here], halo_ref.at[here], halo_sem.at[i]))
+    parts = []
+    for i in range(steps):
+        here = pl.ds(i * part, part)
+        some = pl.ds(i * count, count)
+        parts.append(
+            (
+                started(adj_hbm.at[some, 1], adj_ref.at[some], part_sem.at[0, i]),
+                started(inner_hbm.at[here], inner_ref.at[here], part_sem.at[1, i]),
+                started(emb_hbm.at[here], emb_ref.at[here], part_sem.at[2, i]),
+            )
+        )
+        if i == 0:
+            ready.append(started(w1b_hbm, w1b_ref, weight_sem.at[0]))
+            ready.append(started(w2_hbm, w2_ref, weight_sem.at[1]))
+    for copy in ready:
+        copy.wait()
+    copies = []
+    for i in range(steps):
+        for copy in parts[i]:
+            copy.wait()
+        here = slice(i * part, (i + 1) * part)
+        totals = []
+        for t in range(i * count, (i + 1) * count):
+            total = jnp.dot(adj_ref[t], halo_ref[slot_ref[t]], preferred_element_type=jnp.float32)
+            totals.append(total.astype(jnp.bfloat16))
+        inner = inner_ref[here, :] + jnp.dot(
+            jnp.concatenate(totals, axis=0), w1b_ref[...], preferred_element_type=jnp.float32
+        )
+        activated = gelu(inner).astype(jnp.bfloat16)
+        result = jnp.dot(activated, w2_ref[...], preferred_element_type=jnp.float32)
+        own = emb_ref[here, :].astype(jnp.float32) + b2_ref[...]
+        result_ref[here, :] = (result + own).astype(jnp.bfloat16)
+        copies.append(started(result_ref.at[here], out_hbm.at[here], out_sem.at[i]))
+    for copy in copies:
+        copy.wait()
 
 
 def update(halo_slot, embedding, adjacency, inner, halo, w1b, w2, b2):
     rows, width = embedding.shape
     tiles, _, tile, _ = adjacency.shape
-    count = 4 if tiles % 4 == 0 else 1
-    part = count * tile
-
-    def all_of(array):
-        return pl.BlockSpec(array.shape, lambda i, *_: (0,) * array.ndim)
-
+    steps = tiles // (4 if tiles % 4 == 0 else 1)
+    anywhere = pl.BlockSpec(memory_space=pl.ANY)
+    vmem, dma = pltpu.VMEM, pltpu.SemaphoreType.DMA
     return pl.pallas_call(
-        functools.partial(update_kernel, count),
-        grid_spec=pltpu.PrefetchScalarGridSpec(
-            num_scalar_prefetch=1,
-            grid=(tiles // count,),
-            in_specs=[
-                pl.BlockSpec((part, width), lambda i, *_: (i, 0)),
-                pl.BlockSpec((count, 1, tile, tile), lambda i, *_: (i, 1, 0, 0)),
-                pl.BlockSpec((part, width), lambda i, *_: (i, 0)),
-                all_of(halo),
-                all_of(w1b),
-                all_of(w2),
-                all_of(b2),
-            ],
-            out_specs=pl.BlockSpec((part, width), lambda i, *_: (i, 0)),
-        ),
+        update_kernel,
         out_shape=jax.ShapeDtypeStruct((rows, width), jnp.bfloat16),
+        in_specs=[pl.BlockSpec(memory_space=pltpu.SMEM)]
+        + [anywhere] * 6
+        + [pl.BlockSpec(memory_space=pltpu.VMEM)],
+        out_specs=anywhere,
+        scratch_shapes=[
+            vmem(embedding.shape, jnp.bfloat16),
+            vmem((tiles, tile, tile), jnp.bfloat16),
+            vmem(inner.shape, jnp.float32),
+            vmem(halo.shape, jnp.bfloat16),
+            vmem(w1b.shape, jnp.bfloat16),
+            vmem(w2.shape, jnp.bfloat16),
+            vmem((rows, width), jnp.bfloat16),
+            dma((3, steps)),
+            dma((4,)),
+            dma((2,)),
+            dma((steps,)),
+        ],
         compiler_params=pltpu.CompilerParams(vmem_limit_bytes=60 * 1024 * 1024),
         name="update",
     )(halo_slot, embedding, adjacency, inner, halo, w1b, w2, b2)

time: 41.1 us -> 42 us (1.022)
  Pallas kernels: 40.4 us -> 41.4 us
    pallas_call x1, Pallas kernels: 7.17 us -> 8.17 us  [update(): pl.pallas_call(update_kernel, out_shape=jax.ShapeDtypeStruct((rows, width...]
where the time goes in v4:
time: 42 us; the launch traced here: 41.4 us
  Pallas kernels  41.4 us (99%)
    pallas_call x1, Pallas kernels, per_device(): pl.pallas_call(functools.partial(gather_kernel, n_dom, n_scen, cap, hot_c...  33.3 us
    pallas_call x1, Pallas kernels, update(): pl.pallas_call(update_kernel, out_shape=jax.ShapeDtypeStruct((rows, width...  8.17 us

profile of v4, /device:TPU:0, one launch (start us, length us, event | category | flops | bytes accessed | tf_op | source)
XLA Modules:
  0.0 41.4 jit_solution(17036990819733970422)
XLA Ops:
  0.0 33.3 %gather.1 = (bf16[16,128,256]{2,1,0:T(8,128)(2,1)}, f32[2560,256]{1,0:T(8,128)}, bf16[256,256]{1,0:T(8,128)(2,1)}, bf16[256,256]{1,0:T(8,128)(2,1)}) custom-call(s32[1,128]{1,0:T(1,128)} %bitcast.10, s32[1,20]{1,0:T(1,128)} %bitcast.11, s32[8,256]{1,0:T(8,128)} %rows_hbm.1, s32[8]{0:T(128)} %count_hbm.1, bf16[20,128,256]{2,1,0:T(8,128)(2,1)} %bitcast.6, ...), custom_call_target="tpu_custom_call" | custom-call | tf_op jit(solution)/shard_map/gather/pallas_call | solution.py:668
  33.3 8.2 %update.1 = bf16[2560,256]{1,0:T(8,128)(2,1)} custom-call(s32[20]{0:T(128)} %slot_ref.1, bf16[2560,256]{1,0:T(8,128)(2,1)} %emb_hbm.1, bf16[20,2,128,128]{3,2,1,0:T(8,128)(2,1)} %adj_hbm.3, f32[2560,256]{1,0:T(8,128)} %get-tuple-element.9.inner_hbm, bf16[16,128,256]{2,1,0:T(8,128)(2,1)} %get-tuple-element.10.halo_hbm, ...), custom_call_target="tpu_custom_call" | custom-call | tf_op jit(solution)/shard_map/update/pallas_call | solution.py:599

commit v5 on v3

v5 whole, which is shorter than its diff:
```python
import functools

import jax
import jax.numpy as jnp
from jax import lax
from jax.experimental import pallas as pl
from jax.experimental.pallas import tpu as pltpu
from jax.sharding import PartitionSpec as P

MESH = pl.DeviceIdType.MESH
LANES = 128
GROUP = 256
PAD = 16


def flipped(index, mask):
    bit = 1
    while bit <= mask:
        if mask & bit:
            index = index + bit * (1 - 2 * ((index // bit) % 2))
        bit *= 2
    return index


def spread(row):
    across = jnp.broadcast_to(row.astype(jnp.float32), (LANES, LANES))
    return across, across.T


def whole_part(values, size):
    return jnp.floor((values + 0.5) * (1.0 / size))


def iota_f32(shape, dim):
    return lax.broadcasted_iota(jnp.int32, shape, dim).astype(jnp.float32)


def picked_rows(column, emb_ref):
    tiles, tile, width = emb_ref.shape
    rows = tiles * tile
    lane = iota_f32(column.shape, 1)
    blocks = [
        jnp.where(column == lane + float(at), 1.0, 0.0).astype(jnp.bfloat16)
        for at in range(0, rows, LANES)
    ]
    return jnp.dot(
        jnp.concatenate(blocks, axis=1),
        emb_ref[...].reshape(rows, width),
        preferred_element_type=jnp.float32,
    ).astype(jnp.bfloat16)


def exchange_kernel(
    n_dom,
    n_scen,
    cap,
    hot_cap,
    ints_ref,
    emb_ref,
    weights_ref,
    halo_ref,
    local_ref,
    drv_ref,
    w1f_ref,
    w2f_ref,
    keys_ref,
    wf_ref,
    out_buf,
    stage,
    myreq,
    reqs,
    reqs_smem,
    mine,
    gat1,
    gat2,
    halo_send,
    halo_recv,
    req_send,
    req_recv,
    loc_send,
    loc_recv,
    d1_send,
    d1_recv,
    d2_send,
    d2_recv,
    wf_send,
    wf_recv,
    own_sem,
):
    d = lax.axis_index("dom")
    s = lax.axis_index("scen")
    tiles, tile, width = emb_ref.shape
    rows = tiles * tile
    per = tiles // n_scen
    per_group = max(1, GROUP // cap)
    n_groups = n_dom // per_group
    drv_rows = n_dom * hot_cap

    def dom_peers(body):
        def step(k, carry):
            body(lax.rem(d + k, n_dom))
            return carry

        lax.fori_loop(1, n_dom, step, 0)

    def scen_peers(body):
        for k in range(n_scen - 1, 0, -1):
            body(flipped(s, k))

    def remote(src, dst, send, recv, where):
        return pltpu.make_async_remote_copy(
            src_ref=src,
            dst_ref=dst,
            send_sem=send,
            recv_sem=recv,
            device_id=where,
            device_id_type=MESH,
        )

    def block(ref, index, size):
        return ref.at[pl.ds(pl.multiple_of(index * size, size), size)]

    def halo_place(index):
        if cap >= tile:
            return halo_ref.at[pl.ds(index * (cap // tile), cap // tile)]
        share = tile // cap
        return halo_ref.at[
            index // share, pl.ds(pl.multiple_of((index % share) * cap, cap), cap)
        ]

    def halo_source(index):
        if cap >= tile:
            return out_buf.at[pl.ds(index * (cap // tile), cap // tile)]
        share = tile // cap
        return out_buf.at[
            index // share, pl.ds(pl.multiple_of((index % share) * cap, cap), cap)
        ]

    def halo_copy(peer, mark):
        return remote(
            halo_source(peer),
            halo_place(mark),
            halo_send.at[peer],
            halo_recv.at[mark],
            {"dom": peer},
        )

    def req_copy(peer, mark):
        return remote(myreq, reqs.at[mark], req_send.at[peer], req_recv.at[mark], {"scen": peer})

    def loc_copy(peer, mark):
        return remote(
            stage.at[pl.ds(peer * per, per)],
            local_ref.at[pl.ds(mark * per, per)],
            loc_send.at[peer],
            loc_recv.at[mark],
            {"scen": peer},
        )

    def d1_copy(peer, mark):
        return remote(
            mine, block(gat1, mark, PAD), d1_send.at[peer], d1_recv.at[mark], {"dom": peer}
        )

    doubling = []
    held, mask = [0], n_scen // 2
    while mask:
        doubling.append([(mask, k) for k in held])
        held, mask = held + [k + mask for k in held], mask // 2

    def doubled(ref, send, recv, mask, k):
        part = block(ref, flipped(s, k), ref.shape[0] // n_scen)
        at = (n_scen // (2 * mask) - 1) + held.index(k)
        return remote(part, part, send.at[at], recv.at[at], {"scen": flipped(s, mask)})

    def arriving(ref, send, recv, mask, k):
        part = block(ref, flipped(s, k + mask), ref.shape[0] // n_scen)
        at = (n_scen // (2 * mask) - 1) + held.index(k)
        return remote(part, part, send.at[at], recv.at[at], {"scen": flipped(s, mask)})

    both_weights = ((wf_ref, wf_send, wf_recv),)
    drivers = ((gat2, d2_send, d2_recv),)

    def start_step(arrays, step):
        for mask, k in doubling[step]:
            for array in arrays:
                doubled(*array, mask, k).start()

    def wait_step(arrays, step):
        for mask, k in doubling[step]:
            for array in arrays:
                arriving(*array, mask, k).wait_recv()

    def sent(arrays):
        for steps in doubling:
            for mask, k in steps:
                for array in arrays:
                    doubled(*array, mask, k).wait_send()

    barrier = pltpu.get_barrier_semaphore()
    dom_peers(
        lambda p: pl.semaphore_signal(
            barrier, inc=1, device_id={"dom": p}, device_id_type=MESH
        )
    )
    scen_peers(
        lambda u: pl.semaphore_signal(
            barrier, inc=1, device_id={"scen": u}, device_id_type=MESH
        )
    )

    square = (LANES, LANES)
    lane = iota_f32(square, 1)
    sub = iota_f32(square, 0)

    n_groups_ints = ints_ref.shape[0] - 1
    across = jnp.broadcast_to(ints_ref[n_groups_ints:, LANES:], square)
    down = across.T
    ilane = lax.broadcasted_iota(jnp.int32, square, 1)
    isub = lax.broadcasted_iota(jnp.int32, square, 0)

    def holder(slots):
        found = jnp.where(slots >= 0, 0, -1)
        for u in range(1, n_scen):
            found = found + jnp.where(slots >= u * tiles, 1, 0)
        return found

    own_a, own_d = holder(across), holder(down)
    same = own_a == own_d
    rank_col = jnp.sum(jnp.where(same & (ilane < isub), 1, 0), axis=1, keepdims=True)
    rank_row = jnp.sum(jnp.where(same & (isub < ilane), 1, 0), axis=0, keepdims=True)
    key_col = jnp.where(isub < tiles, own_d * per + rank_col, -1)
    wanted = jnp.sum(
        jnp.where(key_col == ilane, down - own_d * tiles, 0), axis=0, keepdims=True
    )
    myreq[...] = jnp.broadcast_to(wanted, myreq.shape)
    keys_ref[...] = jnp.broadcast_to(own_a[0:1, :] * per + rank_row, keys_ref.shape)

    pl.semaphore_wait(barrier, n_dom - 1 + n_scen - 1)
    scen_peers(lambda u: req_copy(u, s).start())
    share = weights_ref.shape[0]
    block(wf_ref, s, share)[...] = weights_ref[...]
    start_step(both_weights, 0)

    def row_of(index, columns):
        block_of = ints_ref[:, columns]
        at = lax.broadcasted_iota(jnp.int32, block_of.shape, 0)
        return jnp.sum(jnp.where(at == index, block_of, 0), axis=0, keepdims=True)

    def halo_group(group):
        columns = [
            spread(row_of(group, slice(at, at + LANES)))[1] for at in range(0, GROUP, LANES)
        ]
        out_buf[pl.ds(group * (GROUP // LANES), GROUP // LANES)] = picked_rows(
            jnp.concatenate(columns, axis=0), emb_ref
        ).reshape(GROUP // LANES, LANES, width)

    def halo_start(group):
        halo_group(group)
        if per_group == 1:
            halo_copy(group, d).start()
            return

        def step(i, carry):
            p = group * per_group + i

            @pl.when(p != d)
            def _():
                halo_copy(p, d).start()

            return carry

        lax.fori_loop(0, per_group, step, 0)

    my_group = d // per_group
    half_way = n_groups // 2
    order = []
    for k in range(half_way - 1, 0, -1):
        far, near = flipped(my_group, k + half_way), flipped(my_group, k)
        order.append(far + (near - far) * (s % 2))
        order.append(near + (far - near) * (s % 2))
    order.append(flipped(my_group, half_way))
    halo_start(order[0])

    scen_peers(lambda u: req_copy(u, u).wait_recv())
    reqs[pl.ds(s, 1)] = myreq[...][None]
    fetch = pltpu.make_async_copy(reqs, reqs_smem, own_sem.at[0])
    fetch.start()
    fetch.wait()

    def stage_for(u):
        for r in range(per):
            slot = reqs_smem[u, 0, s * per + r]
            stage[pl.ds(u * per + r, 1)] = emb_ref[slot][None]

    def serve(u):
        stage_for(u)
        loc_copy(u, s).start()

    scen_peers(serve)
    stage_for(s)
    local_ref[pl.ds(s * per, per)] = stage[pl.ds(s * per, per)]

    halo_start(order[1])

    r_ids, c_ids = spread(ints_ref[n_groups_ints:, :LANES])
    r_own, c_own = whole_part(r_ids, rows), whole_part(c_ids, rows)
    equal = r_ids == c_ids
    new_col = 1.0 - jnp.max(jnp.where(equal & (lane < sub), 1.0, 0.0), axis=1, keepdims=True)
    new_row = 1.0 - jnp.max(jnp.where(equal & (sub < lane), 1.0, 0.0), axis=0, keepdims=True)
    alike = r_own == c_own
    hot_rank_row = jnp.sum(
        jnp.where(alike & (c_ids < r_ids), new_col, 0.0), axis=0, keepdims=True
    )
    hot_rank_col = jnp.sum(
        jnp.where(alike & (r_ids < c_ids), new_row, 0.0), axis=1, keepdims=True
    )
    me = (d * n_scen + s).astype(jnp.float32)
    own_rows = picked_rows(c_ids - me * float(rows), emb_ref)
    chosen = jnp.where(
        (iota_f32((PAD, LANES), 0) == hot_rank_row) & (r_own[0:1, :] == me), new_row, 0.0
    ).astype(jnp.bfloat16)
    mine[...] = jnp.dot(chosen, own_rows, preferred_element_type=jnp.float32).astype(jnp.bfloat16)
    block(gat1, d, PAD)[...] = mine[...]
    dom_peers(lambda p: d1_copy(p, d).start())

    for group in order[2:]:
        halo_start(group)
    if per_group == 1:
        halo_group(my_group)
    else:
        halo_start(my_group)
    halo_place(d)[...] = halo_source(d)[...]

    wait_step(both_weights, 0)
    start_step(both_weights, 1)

    dom_peers(lambda p: d1_copy(p, p).wait_recv())
    at_row = iota_f32((drv_rows, n_dom * PAD), 0)
    at_dom = whole_part(at_row, hot_cap)
    keep = at_dom * float(PAD) + (at_row - at_dom * float(hot_cap))
    keep = jnp.where(keep == iota_f32(keep.shape, 1), 1.0, 0.0).astype(jnp.bfloat16)
    block(gat2, s, drv_rows)[...] = jnp.dot(
        keep, gat1[...], preferred_element_type=jnp.float32
    ).astype(jnp.bfloat16)
    for step in range(len(doubling)):
        start_step(drivers, step)
        wait_step(drivers, step)
    c_dom = whole_part(c_own, n_scen)
    place = (c_own - c_dom * float(n_scen)) * float(drv_rows) + c_dom * float(hot_cap) + hot_rank_col
    total = jnp.zeros(drv_ref.shape, jnp.float32)
    for at in range(0, n_scen * drv_rows, LANES):
        pick = jnp.where(place == lane + float(at), 1.0, 0.0).astype(jnp.bfloat16)
        total += jnp.dot(pick, gat2[at : at + LANES, :], preferred_element_type=jnp.float32)
    drv_ref[...] = total.astype(jnp.bfloat16)


    for step in range(1, len(doubling)):
        wait_step(both_weights, step)
        if step + 1 < len(doubling):
            start_step(both_weights, step + 1)
    first = w1f_ref.shape[0] // n_scen
    second = w2f_ref.shape[0] // n_scen
    for u in range(n_scen):
        w1f_ref[u * first : (u + 1) * first, :] = wf_ref[u * share : u * share + first, :]
        w2f_ref[u * second : (u + 1) * second, :] = wf_ref[
            u * share + first : (u + 1) * share, :
        ]

    scen_peers(lambda u: loc_copy(u, u).wait())
    dom_peers(lambda p: d1_copy(p, p).wait_send())
    scen_peers(lambda u: req_copy(u, u).wait_send())
    sent(both_weights)
    sent(drivers)
    dom_peers(lambda p: halo_copy(p, p).wait())


def gelu(x):
    size = jnp.abs(x)
    t = 1.0 / (1.0 + (0.3275911 * 0.5**0.5) * size)
    tail = 0.5 * 1.061405429
    for factor in (-1.453152027, 1.421413741, -0.284496736, 0.254829592):
        tail = tail * t + 0.5 * factor
    tail = tail * t * jnp.exp2(x * x * (-0.5 * 1.4426950408889634))
    return jnp.maximum(x, 0.0) - size * tail


def update_kernel(
    keys_ref,
    slot_ref,
    emb_ref,
    feats_ref,
    adj_ref,
    dw_ref,
    halo_ref,
    local_ref,
    drv_ref,
    w1_ref,
    fw_ref,
    b1_ref,
    w2_ref,
    b2_ref,
    out_hbm,
    result_ref,
    out_sem,
):
    tiles, _, tile, _ = adj_ref.shape
    width = emb_ref.shape[1]
    count = 4 if tiles % 4 == 0 else 1
    part = count * tile
    copies = []
    for i in range(tiles // count):
        here = slice(i * part, (i + 1) * part)
        totals = []
        for t in range(i * count, (i + 1) * count):
            rows = slice(t * tile, (t + 1) * tile)
            weights = jnp.concatenate([adj_ref[t, 0], adj_ref[t, 1]], axis=1)
            sources = jnp.concatenate([local_ref[keys_ref[0, t]], halo_ref[slot_ref[t]]], axis=0)
            total = jnp.dot(weights, sources, preferred_element_type=jnp.float32)
            total += jnp.dot(dw_ref[rows, :], drv_ref[...], preferred_element_type=jnp.float32)
            totals.append(total.astype(jnp.bfloat16))
        own = emb_ref[here, :]
        joined = jnp.concatenate([own, jnp.concatenate(totals, axis=0)], axis=1)
        inner = jnp.dot(joined, w1_ref[...], preferred_element_type=jnp.float32)
        inner += lax.dot_general(
            feats_ref[:, here],
            fw_ref[...],
            (((0,), (0,)), ((), ())),
            preferred_element_type=jnp.float32,
        )
        activated = gelu(inner + b1_ref[...]).astype(jnp.bfloat16)
        result = jnp.dot(activated, w2_ref[...], preferred_element_type=jnp.float32)
        result_ref[here, :] = (result + (own.astype(jnp.float32) + b2_ref[...])).astype(
            jnp.bfloat16
        )
        copies.append(
            pltpu.make_async_copy(result_ref.at[here], out_hbm.at[here], out_sem.at[i])
        )
        copies[-1].start()
    for copy in copies:
        copy.wait()


def update(keys, halo_slot, embedding, *rest):
    rows, width = embedding.shape
    vmem = pl.BlockSpec(memory_space=pltpu.VMEM)
    smem = pl.BlockSpec(memory_space=pltpu.SMEM)
    tiles = halo_slot.shape[0]
    return pl.pallas_call(
        update_kernel,
        out_shape=jax.ShapeDtypeStruct((rows, width), jnp.bfloat16),
        in_specs=[smem, smem, vmem] + [vmem] * len(rest),
        out_specs=pl.BlockSpec(memory_space=pl.ANY),
        scratch_shapes=[
            pltpu.VMEM((rows, width), jnp.bfloat16),
            pltpu.SemaphoreType.DMA((tiles,)),
        ],
        compiler_params=pltpu.CompilerParams(vmem_limit_bytes=20 * 1024 * 1024),
        name="update",
    )(keys, halo_slot, embedding, *rest)


def per_device(
    embedding,
    scenario_feats,
    adjacency,
    driver_weight,
    local_slot,
    halo_slot,
    send_rows,
    send_count,
    hot_ids,
    first_weight,
    feature_weight,
    first_bias,
    second_weight,
    second_bias,
):
    n_dom, n_scen = lax.axis_size("dom"), lax.axis_size("scen")
    rows, width = embedding.shape
    tiles, _, tile, _ = adjacency.shape
    slots, cap = send_rows.size, send_rows.shape[1]
    hot = hot_ids.shape[0]
    hot_cap = -(-hot // (n_dom * n_scen))
    assert hot_cap <= PAD and tile == LANES
    bf16, i32 = jnp.bfloat16, jnp.int32
    vmem, smem, dma = pltpu.VMEM, pltpu.SMEM, pltpu.SemaphoreType.DMA
    live = jnp.arange(cap, dtype=i32)[None, :] < send_count[:, None]
    asked = jnp.concatenate([hot_ids, local_slot, jnp.full((LANES - tiles,), -1, i32)])
    ints = jnp.concatenate(
        [jnp.where(live, send_rows, -1).reshape(-1, GROUP), asked.reshape(1, GROUP)], axis=0
    )
    weights = jnp.concatenate([first_weight, second_weight], axis=0)
    in_vmem = pl.BlockSpec(memory_space=pltpu.VMEM)
    by_dom = [dma((n_dom,)), dma((n_dom,))]
    by_scen = [dma((n_scen,)), dma((n_scen,))]
    halo, local, drivers, w1, w2, keys = pl.pallas_call(
        functools.partial(exchange_kernel, n_dom, n_scen, cap, hot_cap),
        out_shape=(
            jax.ShapeDtypeStruct((slots // tile, tile, width), bf16),
            jax.ShapeDtypeStruct((tiles, tile, width), bf16),
            jax.ShapeDtypeStruct((hot, width), bf16),
            jax.ShapeDtypeStruct((n_scen * first_weight.shape[0], width), bf16),
            jax.ShapeDtypeStruct((n_scen * second_weight.shape[0], width), bf16),
            jax.ShapeDtypeStruct((8, LANES), i32),
        ),
        in_specs=[in_vmem] * 3,
        out_specs=(in_vmem,) * 6,
        scratch_shapes=[
            vmem((n_scen * weights.shape[0], width), bf16),
            vmem((slots // tile, tile, width), bf16),
            vmem((tiles, tile, width), bf16),
            vmem((8, LANES), i32),
            vmem((n_scen, 8, LANES), i32),
            smem((n_scen, 8, LANES), i32),
            vmem((PAD, width), bf16),
            vmem((n_dom * PAD, width), bf16),
            vmem((n_scen * n_dom * hot_cap, width), bf16),
            *by_dom,
            *by_scen,
            *by_scen,
            *by_dom,
            *by_scen,
            *by_scen,
            dma((2,)),
        ],
        compiler_params=pltpu.CompilerParams(
            collective_id=0, has_side_effects=True, vmem_limit_bytes=20 * 1024 * 1024
        ),
        cost_estimate=pl.CostEstimate(
            flops=2 * slots * rows * width, bytes_accessed=64 * rows * width, transcendentals=0
        ),
        name="exchange",
    )(ints, embedding.reshape(tiles, tile, width), weights)
    return update(
        keys,
        halo_slot,
        embedding,
        scenario_feats,
        adjacency,
        driver_weight,
        halo,
        local,
        drivers,
        w1,
        feature_weight,
        first_bias.reshape(1, -1),
        w2,
        second_bias.reshape(1, -1),
    )


def solution(mesh):
    return jax.shard_map(
        per_device,
        mesh=mesh,
        in_specs=(
            P(("dom", "scen"), None),
            P(None, ("dom", "scen")),
            P(("dom", "scen"), None, None, None),
            P(("dom", "scen"), None),
            P(("dom", "scen")),
            P(("dom", "scen")),
            P(("dom", "scen"), None),
            P(("dom", "scen")),
            P(),
            P("scen", None),
            P(),
            P(),
            P("scen", None),
            P(),
        ),
        out_specs=P(("dom", "scen"), None),
        check_vma=False,
    )
```

time: 41.1 us -> 42.7 us (1.039)
  other arithmetic: 0 us -> 2.39 us
  Pallas kernels: 40.4 us -> 38.2 us
  local copies, waits for them, and re-layouts: 0 us -> 1.35 us
    pallas_call x2, Pallas kernels: 40.4 us -> 38.2 us  [the longest x1 32.8 us: per_device(): pl.pallas_call(functools.partial(exchange_kernel, n_dom, n_scen, cap, hot...]
    concatenate x0 -> x3, other arithmetic: none -> 1.62 us  [the longest x1 0.87 us: per_device(): weights = jnp.concatenate([first_weight, second_weight], axis=0)]
    unnamed x0 -> x18, local copies, waits for them, and re-layouts: none -> 1.35 us
    select_n x0 -> x1, other arithmetic: none -> 0.77 us  [per_device(): jnp.where(live, send_rows, -1).reshape(-1, GROUP)]
where the time goes in v5:
time: 42.7 us; the launch traced here: 42 us
  Pallas kernels  38.2 us (89%)
  other arithmetic  2.39 us (6%)
  local copies, waits for them, and re-layouts  1.35 us (3%)
    pallas_call x1, Pallas kernels, per_device(): pl.pallas_call(functools.partial(exchange_kernel, n_dom, n_scen, cap, hot...  32.8 us
    pallas_call x1, Pallas kernels, update(): pl.pallas_call(update_kernel, out_shape=jax.ShapeDtypeStruct((rows, width...  5.43 us
    unnamed x18, local copies, waits for them, and re-layouts  1.35 us
    concatenate x1, other arithmetic, per_device(): weights = jnp.concatenate([first_weight, second_weight], axis=0)  0.87 us

profile of v5, /device:TPU:0, one launch (start us, length us, event | category | flops | bytes accessed | tf_op | source)
XLA Modules:
  0.0 42.0 jit_solution(3966519146378360403)
XLA Ops:
  0.0 0.7 %pad_add_fusion.1 = s32[256]{0:T(256)S(1)} fusion(s32[108]{0:T(128)S(1)} %broadcast_in_dim.10, s32[20]{0:T(128)} %param.18, s32[128]{0:T(128)} %param.22), kind=kLoop, calls=%fused_computation.4 | loop fusion | flops 512 | bytes 2048 | tf_op jit(solution)/shard_map/concatenate | solution.py:489
  0.7 0.8 %fusion = s32[8,256]{1,0:T(8,128)S(1)} fusion(s32[8,256]{1,0:T(8,128)} %param.20, s32[8]{0:T(128)} %param.21), kind=kLoop, calls=%fused_computation.3 | loop fusion | flops 4096 | bytes 16416 | tf_op jit(solution)/shard_map/jit(_where)/select_n | solution.py:491
  1.5 0.9 %pad_maximum_fusion.weights_ref = bf16[192,256]{1,0:T(8,128)(2,1)S(1)} fusion(bf16[64,256]{1,0:T(8,128)(2,1)} %param.26, bf16[128,256]{1,0:T(8,128)(2,1)} %param.23), kind=kLoop, calls=%fused_computation | loop fusion | flops 196608 | bytes 196608 | tf_op jit(solution)/shard_map/concatenate | solution.py:493
  2.4 0.0 copy-start
  2.4 1.3 %copy-done = bf16[2560,256]{1,0:T(8,128)(2,1)S(1)} copy-done((bf16[2560,256]{1,0:T(8,128)(2,1)S(1)}, bf16[2560,256]{1,0:T(8,128)(2,1)}, u32[]{:S(2)}) %copy-start) | copy-done | bytes 1310744
  3.7 0.0 copy-start.1
  3.7 0.0 copy-start.2
  3.7 0.0 copy-start.3
  3.7 0.0 copy-start.4
  3.7 0.0 copy-start.5
  3.7 0.0 copy-start.6
  3.7 0.0 copy-start.7
  3.8 0.0 copy-start.8
  3.8 32.8 %exchange.1 = (bf16[16,128,256]{2,1,0:T(8,128)(2,1)S(1)}, bf16[20,128,256]{2,1,0:T(8,128)(2,1)S(1)}, bf16[128,256]{1,0:T(8,128)(2,1)S(1)}, bf16[512,256]{1,0:T(8...) custom-call(s32[9,256]{1,0:T(8,128)S(1)} %pad_add_fusion.ints_ref, bf16[20,128,256]{2,1,0:T(8,128)(2,1)S(1)} %bitcast.4, ...), custom_call_target="tpu_custom_call" | custom-call | flops 2684354560 | bytes 41943040 | tf_op jit(solution)/shard_map/exchange/pallas_call | solution.py:497
  36.5 0.0 copy-done.1
  36.5 0.0 copy-done.2
  36.6 0.0 copy-done.3
  36.6 0.0 copy-done.4
  36.6 0.0 copy-done.5
  36.6 0.0 copy-done.6
  36.6 0.0 copy-done.7
  36.6 0.0 copy-done.8
  36.6 5.4 %update.1 = bf16[2560,256]{1,0:T(8,128)(2,1)} custom-call(s32[8,128]{1,0:T(8,128)S(1)} %get-tuple-element.11.keys_ref, s32[20]{0:T(128)S(1)} %copy-done.8, bf16[2560,256]{1,0:T(8,128)(2,1)S(1)} %copy-done.1, bf16[16,2560]{1,0:T(8,128)(2,1)S(1)} %copy-done.4, bf16[20,2,128,128]{3,2,1,0:T(8,128)(2,1)S(1)} %copy-done.2, bf16[2560,128]{1,0:T(8,128)(2,1)S(1)} %copy-done.3, ...), custom_call_target="tpu_custom_call" | custom-call | tf_op jit(solution)/shard_map/update/pallas_call | solution.py:449
  (2 shorter events, 0.0 us)
Async XLA Ops:
  2.4 1.3 %copy-start = (bf16[2560,256]{1,0:T(8,128)(2,1)S(1)}, bf16[2560,256]{1,0:T(8,128)(2,1)}, u32[]{:S(2)}) copy-start(bf16[2560,256]{1,0:T(8,128)(2,1)} %emb_ref.1) | copy-start | bytes 3932164
  3.7 32.8 %copy-start.1 = (bf16[2560,256]{1,0:T(8,128)(2,1)S(1)}, bf16[2560,256]{1,0:T(8,128)(2,1)}, u32[]{:S(2)}) copy-start(bf16[2560,256]{1,0:T(8,128)(2,1)} %emb_ref.1) | copy-start | bytes 3932164
  3.7 32.8 %copy-start.2 = (bf16[20,2,128,128]{3,2,1,0:T(8,128)(2,1)S(1)}, bf16[20,2,128,128]{3,2,1,0:T(8,128)(2,1)}, u32[]{:S(2)}) copy-start(bf16[20,2,128,128]{3,2,1,0:T(8,128)(2,1)} %adj_ref.1) | copy-start | bytes 3932164
  3.7 32.8 %copy-start.3 = (bf16[2560,128]{1,0:T(8,128)(2,1)S(1)}, bf16[2560,128]{1,0:T(8,128)(2,1)}, u32[]{:S(2)}) copy-start(bf16[2560,128]{1,0:T(8,128)(2,1)} %dw_ref.1) | copy-start | bytes 1966084
  3.7 32.8 %copy-start.4 = (bf16[16,2560]{1,0:T(8,128)(2,1)S(1)}, bf16[16,2560]{1,0:T(8,128)(2,1)}, u32[]{:S(2)}) copy-start(bf16[16,2560]{1,0:T(8,128)(2,1)} %feats_ref.1) | copy-start | bytes 245764
  3.7 32.9 %copy-start.5 = (bf16[16,256]{1,0:T(8,128)(2,1)S(1)}, bf16[16,256]{1,0:T(8,128)(2,1)}, u32[]{:S(2)}) copy-start(bf16[16,256]{1,0:T(8,128)(2,1)} %fw_ref.1) | copy-start | bytes 24580
  3.7 32.9 %copy-start.6 = (f32[256]{0:T(256)S(1)}, f32[256]{0:T(256)}, u32[]{:S(2)}) copy-start(f32[256]{0:T(256)} %param.25) | copy-start | bytes 3076
  3.7 32.8 %copy-start.7 = (f32[256]{0:T(256)S(1)}, f32[256]{0:T(256)}, u32[]{:S(2)}) copy-start(f32[256]{0:T(256)} %param.27) | copy-start | bytes 3076
  3.8 32.8 %copy-start.8 = (s32[20]{0:T(128)S(1)}, s32[20]{0:T(128)}, u32[]{:S(2)}) copy-start(s32[20]{0:T(128)} %slot_ref.1) | copy-start | bytes 244

commit v6 on v3

--- a/solution.py
+++ b/solution.py
@@ -420,10 +420,6 @@
     for step in range(len(doubling)):
         start_step(drivers, step)
         wait_step(drivers, step)
-    for step in range(1, len(doubling)):
-        wait_step(both_weights, step)
-        if step + 1 < len(doubling):
-            start_step(both_weights, step + 1)
     c_dom = whole_part(c_own, n_scen)
     place = (c_own - c_dom * float(n_scen)) * float(drv_rows) + c_dom * float(hot_cap) + hot_rank_col
     total = jnp.zeros(drv_ref.shape, jnp.float32)
@@ -433,8 +429,33 @@
     drv_ref[...] = total.astype(jnp.bfloat16)
 
 
+    for step in range(1, len(doubling)):
+        wait_step(both_weights, step)
+        if step + 1 < len(doubling):
+            start_step(both_weights, step + 1)
     for name in ("feats", "fw", "b1", "dw", "adj"):
         loads[name].wait()
+    count = 4 if tiles % 4 == 0 else 1
+    part = count * tile
+
+    def own_part(i, carry):
+        here = pl.ds(pl.multiple_of(i * part, part), part)
+        inner = jnp.dot(
+            emb_ref[pl.ds(i * count, count)].reshape(part, width),
+            w1f_ref[:width, :],
+            preferred_element_type=jnp.float32,
+        )
+        inner += lax.dot_general(
+            feats_ref[:, here],
+            fw_ref[...],
+            (((0,), (0,)), ((), ())),
+            preferred_element_type=jnp.float32,
+        )
+        inner_ref[here, :] = inner + b1_ref[...]
+        return carry
+
+    lax.fori_loop(0, tiles // count, own_part, 0)
+
     scen_peers(lambda u: loc_copy(u, u).wait())
     to_out = [
         pltpu.make_async_copy(w1f_ref.at[pl.ds(width, width)], w1b_hbm, own_sem.at[3]),
@@ -445,26 +466,13 @@
     keys_copy = pltpu.make_async_copy(keys_ref, keys_smem, own_sem.at[1])
     keys_copy.start()
     keys_copy.wait()
-    count = 4 if tiles % 4 == 0 else 1
-    part = count * tile
 
     def inner_copy(i):
         here = pl.ds(pl.multiple_of(i * part, part), part)
         return pltpu.make_async_copy(inner_ref.at[here], inner_hbm.at[here], inner_sem.at[i])
 
-    def own_part(i, carry):
+    def local_part(i, carry):
         here = pl.ds(pl.multiple_of(i * part, part), part)
-        inner = jnp.dot(
-            emb_ref[pl.ds(i * count, count)].reshape(part, width),
-            w1f_ref[:width, :],
-            preferred_element_type=jnp.float32,
-        )
-        inner += lax.dot_general(
-            feats_ref[:, here],
-            fw_ref[...],
-            (((0,), (0,)), ((), ())),
-            preferred_element_type=jnp.float32,
-        )
         totals = []
         for j in range(count):
             t = i * count + j
@@ -472,16 +480,15 @@
             sources = jnp.concatenate([local_ref[keys_smem[0, t]], drv_ref[...]], axis=0)
             total = jnp.dot(weights, sources, preferred_element_type=jnp.float32)
             totals.append(total.astype(jnp.bfloat16))
-        inner += jnp.dot(
+        inner_ref[here, :] += jnp.dot(
             jnp.concatenate(totals, axis=0),
             w1f_ref[width:, :],
             preferred_element_type=jnp.float32,
         )
-        inner_ref[here, :] = inner + b1_ref[...]
         inner_copy(i).start()
         return carry
 
-    lax.fori_loop(0, tiles // count, own_part, 0)
+    lax.fori_loop(0, tiles // count, local_part, 0)
 
     dom_peers(lambda p: d1_copy(p, p).wait_send())
     scen_peers(lambda u: req_copy(u, u).wait_send())
@@ -500,48 +507,104 @@
 
 
 def update_kernel(
-    count, slot_ref, emb_ref, adj_ref, inner_ref, halo_ref, w1b_ref, w2_ref, b2_ref, out_ref
+    count,
+    slot_ref,
+    emb_hbm,
+    adj_hbm,
+    inner_hbm,
+    halo_hbm,
+    w1b_hbm,
+    w2_hbm,
+    b2_ref,
+    out_ref,
+    emb_ref,
+    adj_ref,
+    inner_ref,
+    halo_ref,
+    w1b_ref,
+    w2_ref,
+    part_sem,
+    whole_sem,
 ):
     step = pl.program_id(0)
+    part = out_ref.shape[0]
+    steps = adj_ref.shape[0] // count
+
+    def part_copies(i):
+        here = pl.ds(pl.multiple_of(i * part, part), part)
+        some = pl.ds(i * count, count)
+        return (
+            pltpu.make_async_copy(adj_hbm.at[some, 1], adj_ref.at[some], part_sem.at[0, i]),
+            pltpu.make_async_copy(inner_hbm.at[here], inner_ref.at[here], part_sem.at[1, i]),
+            pltpu.make_async_copy(emb_hbm.at[here], emb_ref.at[here], part_sem.at[2, i]),
+        )
+
+    half = halo_ref.shape[0] // 2
+    whole_copies = [
+        pltpu.make_async_copy(
+            halo_hbm.at[pl.ds(at * half, half)], halo_ref.at[pl.ds(at * half, half)], whole_sem.at[at]
+        )
+        for at in range(2)
+    ]
+    whole_copies.append(pltpu.make_async_copy(w1b_hbm, w1b_ref, whole_sem.at[2]))
+    whole_copies.append(pltpu.make_async_copy(w2_hbm, w2_ref, whole_sem.at[3]))
+
+    @pl.when(step == 0)
+    def _():
+        for copy in whole_copies:
+            copy.start()
+        for i in range(min(2, steps)):
+            for copy in part_copies(i):
+                copy.start()
+        for copy in whole_copies:
+            copy.wait()
+
+    @pl.when(step + 2 < steps)
+    def _():
+        for copy in part_copies(step + 2):
+            copy.start()
+
+    for copy in part_copies(step):
+        copy.wait()
+    here = pl.ds(pl.multiple_of(step * part, part), part)
     totals = []
     for j in range(count):
-        halo = halo_ref[slot_ref[step * count + j]]
-        total = jnp.dot(adj_ref[j, 0], halo, preferred_element_type=jnp.float32)
+        t = step * count + j
+        total = jnp.dot(adj_ref[t], halo_ref[slot_ref[t]], preferred_element_type=jnp.float32)
         totals.append(total.astype(jnp.bfloat16))
-    inner = inner_ref[...] + jnp.dot(
+    inner = inner_ref[here, :] + jnp.dot(
         jnp.concatenate(totals, axis=0), w1b_ref[...], preferred_element_type=jnp.float32
     )
     activated = (0.5 * inner * (1.0 + lax.erf(inner * (0.5**0.5)))).astype(jnp.bfloat16)
     result = jnp.dot(activated, w2_ref[...], preferred_element_type=jnp.float32)
-    out_ref[...] = (result + (emb_ref[...].astype(jnp.float32) + b2_ref[...])).astype(
-        jnp.bfloat16
-    )
+    own = emb_ref[here, :].astype(jnp.float32) + b2_ref[...]
+    out_ref[...] = (result + own).astype(jnp.bfloat16)
 
 
 def update(halo_slot, embedding, adjacency, inner, halo, w1b, w2, b2):
     rows, width = embedding.shape
     tiles, _, tile, _ = adjacency.shape
     count = 4 if tiles % 4 == 0 else 1
-    part = count * tile
-
-    def all_of(array):
-        return pl.BlockSpec(array.shape, lambda i, *_: (0,) * array.ndim)
-
+    steps = tiles // count
+    anywhere = pl.BlockSpec(memory_space=pl.ANY)
+    vmem, dma = pltpu.VMEM, pltpu.SemaphoreType.DMA
     return pl.pallas_call(
         functools.partial(update_kernel, count),
         grid_spec=pltpu.PrefetchScalarGridSpec(
             num_scalar_prefetch=1,
-            grid=(tiles // count,),
-            in_specs=[
-                pl.BlockSpec((part, width), lambda i, *_: (i, 0)),
-                pl.BlockSpec((count, 1, tile, tile), lambda i, *_: (i, 1, 0, 0)),
-                pl.BlockSpec((part, width), lambda i, *_: (i, 0)),
-                all_of(halo),
-                all_of(w1b),
-                all_of(w2),
-                all_of(b2),
+            grid=(steps,),
+            in_specs=[anywhere] * 6 + [pl.BlockSpec(b2.shape, lambda i, *_: (0, 0))],
+            out_specs=pl.BlockSpec((count * tile, width), lambda i, *_: (i, 0)),
+            scratch_shapes=[
+                vmem(embedding.shape, jnp.bfloat16),
+                vmem((tiles, tile, tile), jnp.bfloat16),
+                vmem(inner.shape, jnp.float32),
+                vmem(halo.shape, jnp.bfloat16),
+                vmem(w1b.shape, jnp.bfloat16),
+                vmem(w2.shape, jnp.bfloat16),
+                dma((3, steps)),
+                dma((4,)),
             ],
-            out_specs=pl.BlockSpec((part, width), lambda i, *_: (i, 0)),
         ),
         out_shape=jax.ShapeDtypeStruct((rows, width), jnp.bfloat16),
         compiler_params=pltpu.CompilerParams(vmem_limit_bytes=60 * 1024 * 1024),

time: 41.1 us -> 41 us (level)
  no operation moved by 1% of the time
where the time goes in v6:
time: 41 us; the launch traced here: 40.4 us
  Pallas kernels  40.4 us (99%)
    pallas_call x1, Pallas kernels, per_device(): pl.pallas_call(functools.partial(gather_kernel, n_dom, n_scen, cap, hot_c...  33.3 us
    pallas_call x1, Pallas kernels, update(): pl.pallas_call(functools.partial(update_kernel, count), grid_spec=pltpu.P...  7.1 us

profile of v6, /device:TPU:0, one launch (start us, length us, event | category | flops | bytes accessed | tf_op | source)
XLA Modules:
  0.0 40.4 jit_solution(859007544921450780)
XLA Ops:
  0.0 33.3 %gather.1 = (bf16[16,128,256]{2,1,0:T(8,128)(2,1)}, f32[2560,256]{1,0:T(8,128)}, bf16[256,256]{1,0:T(8,128)(2,1)}, bf16[256,256]{1,0:T(8,128)(2,1)}) custom-call(s32[1,128]{1,0:T(1,128)} %bitcast.10, s32[1,20]{1,0:T(1,128)} %bitcast.11, s32[8,256]{1,0:T(8,128)} %rows_hbm.1, s32[8]{0:T(128)} %count_hbm.1, bf16[20,128,256]{2,1,0:T(8,128)(2,1)} %bitcast.6, ...), custom_call_target="tpu_custom_call" | custom-call | tf_op jit(solution)/shard_map/gather/pallas_call | solution.py:659
  33.3 7.1 %update.1 = bf16[2560,256]{1,0:T(8,128)(2,1)} custom-call(s32[20]{0:T(128)} %slot_ref.1, bf16[2560,256]{1,0:T(8,128)(2,1)} %emb_hbm.1, bf16[20,2,128,128]{3,2,1,0:T(8,128)(2,1)} %adj_hbm.3, f32[2560,256]{1,0:T(8,128)} %get-tuple-element.9.inner_hbm, bf16[16,128,256]{2,1,0:T(8,128)(2,1)} %get-tuple-element.10.halo_hbm, ...), custom_call_target="tpu_custom_call" | custom-call | tf_op jit(solution)/shard_map/update/pallas_call | solution.py:591
